TPU v7x, 32 devices: a whole 2x2x4 slice. The times are simulated.
32 devices in a mesh: grp: 4 (over x, core), seq: 8 (over z, y).
Axes of the slice: x: 2, y: 2, z: 4, core: 2. Of those that a mesh axis runs over, the one named last changes fastest.
Arguments:
- tokens: bfloat16 [8, 512, 1280], P('grp', 'seq'), may hold values from -6 to 6
- lengths: int32 [8], P('grp'), may hold values from 128 to 512, as said below
- query_weight: bfloat16 [1280, 1280], P(('grp', 'seq')), may hold values from -0.15625 to 0.15625
- key_weight: bfloat16 [1280, 1280], P(('grp', 'seq')), may hold values from -0.15625 to 0.15625
- value_weight: bfloat16 [1280, 1280], P(('grp', 'seq')), may hold values from -0.15625 to 0.15625
- out_weight: bfloat16 [1280, 1280], P(('grp', 'seq')), may hold values from -0.5 to 0.5
- up_weight: bfloat16 [1280, 1280], P(('grp', 'seq')), may hold values from -0.15625 to 0.15625
- down_weight: bfloat16 [1280, 1280], P(('grp', 'seq')), may hold values from -0.15625 to 0.15625
- norm_gain: bfloat16 [1280], P(('grp', 'seq')), may hold values from 0.099609375 to 1.8984375
- ff_gain: bfloat16 [1280], P(('grp', 'seq')), may hold values from 0.099609375 to 1.8984375
- up_bias: bfloat16 [1280], P(('grp', 'seq')), may hold values from -3 to 3
- down_bias: bfloat16 [1280], P(('grp', 'seq')), may hold values from -3 to 3
- query_scale: float32 [80], replicated, may hold values from -1 to 1
- cotangent: bfloat16 [8, 512, 1280], P('grp', 'seq'), may hold values from -6 to 6
Outputs:
- activations: bfloat16 [8, 512, 1280], P('grp', 'seq')
- grad_tokens: float32 [8, 512, 1280], P('grp', 'seq')
- grad_query_weight: float32 [1280, 1280], P('seq')
- grad_key_weight: float32 [1280, 1280], P('seq')
- grad_value_weight: float32 [1280, 1280], P('seq')
- grad_out_weight: float32 [1280, 1280], P('seq')
- grad_up_weight: float32 [1280, 1280], P('seq')
- grad_down_weight: float32 [1280, 1280], P('seq')
- grad_norm_gain: float32 [1280], replicated
- grad_ff_gain: float32 [1280], replicated
- grad_up_bias: float32 [1280], replicated
- grad_down_bias: float32 [1280], replicated
- grad_query_scale: float32 [80], replicated
Inputs may be any that keep to these rules, and one draw needn't show every extreme that they name: `lengths`: on each index of grp, one of its 2 sequences has all 512 tokens valid.
All inputs are finite; a program needn't handle non-finite values.
Results may differ from a plain program's by a relative error of at most 0.014.
Values may be sent and summed in bfloat16 or wider, within the bound.
No kernel may reach another device: no remote copies, remote signals or barrier semaphores. Data moves between devices by JAX's collectives and lax.ppermute only.
A program may use at most 192 MiB of HBM per device.

v0:
```python
import math

import jax
import jax.numpy as jnp
from jax import lax
from jax.sharding import PartitionSpec as P

EPS = 1e-06
QCONST = 1.442695041
NEG = -1e30


def heads_of(array, head_size):
    return array.reshape(array.shape[0], array.shape[1], array.shape[2] // head_size, head_size)


def masked_scores(query_rows, query_pos, key_rows, key_pos, lengths, head_size):
    scores = jnp.einsum(
        "sqhe,skhe->shqk",
        heads_of(query_rows, head_size),
        heads_of(key_rows, head_size),
        preferred_element_type=jnp.float32,
    )
    allowed = (key_pos[None, None, :] <= query_pos[None, :, None]) & (
        key_pos[None, None, :] < lengths[:, None, None]
    )
    allowed = allowed[:, None]
    return (jnp.where(allowed, scores, NEG), allowed)


def over_blocks(carry, pieces, update):
    count = pieces[0].shape[1]
    block = math.gcd(count, 512)

    def inner(state, number):
        offset = number * block
        parts = tuple((lax.dynamic_slice_in_dim(piece, offset, block, 1) for piece in pieces))
        return (update(state, parts, offset), None)

    carry, _ = lax.scan(inner, carry, jnp.arange(count // block, dtype=jnp.int32))
    return carry


def shards(
    tokens,
    lengths,
    query_weight,
    key_weight,
    value_weight,
    out_weight,
    up_weight,
    down_weight,
    norm_gain,
    ff_gain,
    up_bias,
    down_bias,
    query_scale,
    cotangent,
):
    seq_count, rows, width = tokens.shape
    head_size = query_scale.shape[0]
    heads = width // head_size
    first = lax.axis_index("seq") * rows
    own_pos = first + jnp.arange(rows, dtype=jnp.int32)
    last_pos = first + rows - 1
    longest = jnp.max(lengths)
    params = (
        query_weight,
        key_weight,
        value_weight,
        out_weight,
        up_weight,
        down_weight,
        norm_gain,
        ff_gain,
        up_bias,
        down_bias,
    )
    whole = (
        lax.all_gather(params[0], ("grp", "seq"), axis=0, tiled=True),
        lax.all_gather(params[1], ("grp", "seq"), axis=0, tiled=True),
        lax.all_gather(params[2], ("grp", "seq"), axis=0, tiled=True),
        lax.all_gather(params[3], ("grp", "seq"), axis=0, tiled=True),
        lax.all_gather(params[4], ("grp", "seq"), axis=0, tiled=True),
        lax.all_gather(params[5], ("grp", "seq"), axis=0, tiled=True),
        lax.all_gather(params[6], ("grp", "seq"), axis=0, tiled=True),
        lax.all_gather(params[7], ("grp", "seq"), axis=0, tiled=True),
        lax.all_gather(params[8], ("grp", "seq"), axis=0, tiled=True),
        lax.all_gather(params[9], ("grp", "seq"), axis=0, tiled=True),
    )
    w_query, w_key, w_value, w_out, w_up, w_down, gain_one, gain_two, bias_up, bias_down = whole
    factor = QCONST / math.sqrt(head_size)
    scale = factor * jax.nn.softplus(query_scale)
    inputs = tokens.astype(jnp.float32)
    inv_one = lax.rsqrt(jnp.mean(inputs * inputs, axis=-1, keepdims=True) + EPS)
    normed = (inputs * inv_one * gain_one.astype(jnp.float32)).astype(jnp.bfloat16)
    query_raw = jnp.einsum("sre,ef->srf", normed, w_query, preferred_element_type=jnp.float32)
    queries = (
        (heads_of(query_raw, head_size) * scale)
        .astype(jnp.bfloat16)
        .reshape(seq_count, rows, width)
    )
    keys = jnp.einsum("sre,ef->srf", normed, w_key, preferred_element_type=jnp.float32).astype(
        jnp.bfloat16
    )
    values = jnp.einsum("sre,ef->srf", normed, w_value, preferred_element_type=jnp.float32).astype(
        jnp.bfloat16
    )

    def peak_update(state, parts, start):
        key_part = parts[0]
        live = (start <= last_pos) & (start < longest)

        def peak_work(current):
            peak, total = current
            key_pos = start + jnp.arange(key_part.shape[1], dtype=jnp.int32)
            scores, allowed = masked_scores(queries, own_pos, key_part, key_pos, lengths, head_size)
            fresh = jnp.maximum(peak, jnp.max(scores, axis=-1))
            weights = jnp.where(allowed, jnp.exp(scores - fresh[..., None]), 0.0)
            return (fresh, total * jnp.exp(peak - fresh) + jnp.sum(weights, axis=-1))

        return lax.cond(live, peak_work, lambda current: current, state)

    stat_shape = (seq_count, heads, rows)
    peak, total = over_blocks(
        (jnp.full(stat_shape, NEG, jnp.float32), jnp.zeros(stat_shape, jnp.float32)),
        (lax.all_gather(keys, "seq", axis=1, tiled=True),),
        peak_update,
    )
    log_total = peak + jnp.log(total)

    def value_update(state, parts, start):
        key_part, value_part = parts
        live = (start <= last_pos) & (start < longest)

        def value_work(current):
            summed, remainder = current
            key_pos = start + jnp.arange(key_part.shape[1], dtype=jnp.int32)
            scores, allowed = masked_scores(queries, own_pos, key_part, key_pos, lengths, head_size)
            probs = jnp.where(allowed, jnp.exp(scores - log_total[..., None]), 0.0)
            rounded = probs.astype(jnp.bfloat16)
            leftover = (probs - rounded.astype(jnp.float32)).astype(jnp.bfloat16)
            value_heads = heads_of(value_part, head_size)
            summed = summed + jnp.einsum(
                "shqk,skhe->sqhe", rounded, value_heads, preferred_element_type=jnp.float32
            )
            remainder = remainder + jnp.einsum(
                "shqk,skhe->sqhe", leftover, value_heads, preferred_element_type=jnp.float32
            )
            return (summed, remainder)

        return lax.cond(live, value_work, lambda current: current, state)

    zero_heads = jnp.zeros((seq_count, rows, heads, head_size), jnp.float32)
    summed, remainder = over_blocks(
        (zero_heads, zero_heads),
        (
            lax.all_gather(keys, "seq", axis=1, tiled=True),
            lax.all_gather(values, "seq", axis=1, tiled=True),
        ),
        value_update,
    )
    attended = summed.reshape(seq_count, rows, width).astype(jnp.bfloat16)
    exact = summed + remainder
    mixed = jnp.einsum("srf,fe->sre", attended, w_out, preferred_element_type=jnp.float32)
    hidden = inputs + mixed
    inv_two = lax.rsqrt(jnp.mean(hidden * hidden, axis=-1, keepdims=True) + EPS)
    normed_two = (hidden * inv_two * gain_two.astype(jnp.float32)).astype(jnp.bfloat16)
    pre = jnp.einsum(
        "sre,ef->srf", normed_two, w_up, preferred_element_type=jnp.float32
    ) + bias_up.astype(jnp.float32)
    act = jax.nn.silu(pre).astype(jnp.bfloat16)
    branch = jnp.einsum("srf,fe->sre", act, w_down, preferred_element_type=jnp.float32)
    layer_out = (hidden + branch + bias_down.astype(jnp.float32)).astype(jnp.bfloat16)
    back = (
        lax.all_gather(params[0], ("grp", "seq"), axis=0, tiled=True),
        lax.all_gather(params[1], ("grp", "seq"), axis=0, tiled=True),
        lax.all_gather(params[2], ("grp", "seq"), axis=0, tiled=True),
        lax.all_gather(params[3], ("grp", "seq"), axis=0, tiled=True),
        lax.all_gather(params[4], ("grp", "seq"), axis=0, tiled=True),
        lax.all_gather(params[5], ("grp", "seq"), axis=0, tiled=True),
        lax.all_gather(params[6], ("grp", "seq"), axis=0, tiled=True),
        lax.all_gather(params[7], ("grp", "seq"), axis=0, tiled=True),
        lax.all_gather(params[8], ("grp", "seq"), axis=0, tiled=True),
        lax.all_gather(params[9], ("grp", "seq"), axis=0, tiled=True),
    )
    back_query, back_key, back_value, back_out, back_up, back_down, back_gain_one, back_gain_two = (
        back[:8]
    )
    valid = own_pos[None, :] < lengths[:, None]
    grad_out = jnp.where(valid[..., None], cotangent, jnp.zeros_like(cotangent))
    grad_down = jnp.einsum("srf,sre->fe", act, grad_out, preferred_element_type=jnp.float32)
    grad_act = jnp.einsum("sre,fe->srf", grad_out, back_down, preferred_element_type=jnp.float32)
    sigma = jax.nn.sigmoid(pre)
    grad_pre = (grad_act * sigma * (1.0 + pre * (1.0 - sigma))).astype(jnp.bfloat16)
    grad_up = jnp.einsum("sre,srf->ef", normed_two, grad_pre, preferred_element_type=jnp.float32)
    grad_normed_two = jnp.einsum(
        "srf,ef->sre", grad_pre, back_up, preferred_element_type=jnp.float32
    )
    grad_gain_two = jnp.sum(grad_normed_two * hidden * inv_two, axis=(0, 1))
    weighted_two = grad_normed_two * back_gain_two.astype(jnp.float32)
    grad_hidden = (
        grad_out.astype(jnp.float32)
        + inv_two * weighted_two
        - hidden
        * (inv_two * inv_two * inv_two)
        * jnp.mean(weighted_two * hidden, axis=-1, keepdims=True)
    )
    grad_mixed = grad_hidden.astype(jnp.bfloat16)
    grad_out_weight = jnp.einsum(
        "srf,sre->fe", attended, grad_mixed, preferred_element_type=jnp.float32
    )
    grad_att = jnp.einsum(
        "sre,fe->srf", grad_mixed, back_out, preferred_element_type=jnp.float32
    ).astype(jnp.bfloat16)
    grad_att_heads = heads_of(grad_att, head_size)
    delta = jnp.einsum("sqhe,sqhe->shq", grad_att_heads.astype(jnp.float32), exact)
    all_log, all_delta = (
        lax.all_gather(log_total, "seq", axis=2, tiled=True),
        lax.all_gather(delta, "seq", axis=2, tiled=True),
    )

    def query_update(state, parts, start):
        key_part, value_part = parts
        live = (start <= last_pos) & (start < longest)

        def query_work(current):
            key_pos = start + jnp.arange(key_part.shape[1], dtype=jnp.int32)
            scores, allowed = masked_scores(queries, own_pos, key_part, key_pos, lengths, head_size)
            probs = jnp.where(allowed, jnp.exp(scores - log_total[..., None]), 0.0)
            grad_probs = jnp.einsum(
                "sqhe,skhe->shqk",
                grad_att_heads,
                heads_of(value_part, head_size),
                preferred_element_type=jnp.float32,
            )
            grad_scores = (probs * (grad_probs - delta[..., None])).astype(jnp.bfloat16)
            return current + jnp.einsum(
                "shqk,skhe->sqhe",
                grad_scores,
                heads_of(key_part, head_size),
                preferred_element_type=jnp.float32,
            )

        return lax.cond(live, query_work, lambda current: current, state)

    grad_query_sum = over_blocks(
        zero_heads,
        (
            lax.all_gather(keys, "seq", axis=1, tiled=True),
            lax.all_gather(values, "seq", axis=1, tiled=True),
        ),
        query_update,
    )
    grad_queries = grad_query_sum.astype(jnp.bfloat16)
    own_values = heads_of(values, head_size)

    def key_update(state, parts, start):
        query_part, grad_part = parts
        count = query_part.shape[1]
        live = (start + count - 1 >= first) & (first < longest)

        def key_work(current):
            grad_key_sum, grad_value_sum = current
            query_pos = start + jnp.arange(count, dtype=jnp.int32)
            scores, allowed = masked_scores(
                query_part, query_pos, keys, own_pos, lengths, head_size
            )
            log_part = lax.dynamic_slice_in_dim(all_log, start, count, 2)
            delta_part = lax.dynamic_slice_in_dim(all_delta, start, count, 2)
            probs = jnp.where(allowed, jnp.exp(scores - log_part[..., None]), 0.0)
            grad_heads = heads_of(grad_part, head_size)
            grad_value_sum = grad_value_sum + jnp.einsum(
                "shqk,sqhe->skhe",
                probs.astype(jnp.bfloat16),
                grad_heads,
                preferred_element_type=jnp.float32,
            )
            grad_probs = jnp.einsum(
                "sqhe,skhe->shqk", grad_heads, own_values, preferred_element_type=jnp.float32
            )
            grad_scores = (probs * (grad_probs - delta_part[..., None])).astype(jnp.bfloat16)
            grad_key_sum = grad_key_sum + jnp.einsum(
                "shqk,sqhe->skhe",
                grad_scores,
                heads_of(query_part, head_size),
                preferred_element_type=jnp.float32,
            )
            return (grad_key_sum, grad_value_sum)

        return lax.cond(live, key_work, lambda current: current, state)

    grad_key_sum, grad_value_sum = over_blocks(
        (zero_heads, zero_heads),
        (
            lax.all_gather(queries, "seq", axis=1, tiled=True),
            lax.all_gather(grad_att, "seq", axis=1, tiled=True),
        ),
        key_update,
    )
    grad_keys = grad_key_sum.reshape(seq_count, rows, width).astype(jnp.bfloat16)
    grad_values = grad_value_sum.reshape(seq_count, rows, width).astype(jnp.bfloat16)
    grad_queries_wide = grad_queries.astype(jnp.float32)
    grad_scale = (
        jnp.sum(grad_queries_wide * heads_of(query_raw, head_size), axis=(0, 1, 2))
        * factor
        * jax.nn.sigmoid(query_scale)
    )
    grad_query_raw = (
        (grad_queries_wide * scale).astype(jnp.bfloat16).reshape(seq_count, rows, width)
    )
    grad_query_w = jnp.einsum(
        "sre,srf->ef", normed, grad_query_raw, preferred_element_type=jnp.float32
    )
    grad_key_w = jnp.einsum("sre,srf->ef", normed, grad_keys, preferred_element_type=jnp.float32)
    grad_value_w = jnp.einsum(
        "sre,srf->ef", normed, grad_values, preferred_element_type=jnp.float32
    )
    grad_normed = (
        jnp.einsum("srf,ef->sre", grad_query_raw, back_query, preferred_element_type=jnp.float32)
        + jnp.einsum("srf,ef->sre", grad_keys, back_key, preferred_element_type=jnp.float32)
        + jnp.einsum("srf,ef->sre", grad_values, back_value, preferred_element_type=jnp.float32)
    )
    grad_gain_one = jnp.sum(grad_normed * inputs * inv_one, axis=(0, 1))
    weighted_one = grad_normed * back_gain_one.astype(jnp.float32)
    grad_tokens = (
        grad_hidden
        + inv_one * weighted_one
        - inputs
        * (inv_one * inv_one * inv_one)
        * jnp.mean(weighted_one * inputs, axis=-1, keepdims=True)
    )
    grad_bias_up = jnp.sum(grad_pre.astype(jnp.float32), axis=(0, 1))
    grad_bias_down = jnp.sum(grad_out.astype(jnp.float32), axis=(0, 1))
    small = lax.psum(
        (grad_gain_one, grad_gain_two, grad_bias_up, grad_bias_down, grad_scale), ("grp", "seq")
    )
    grads = (grad_query_w, grad_key_w, grad_value_w, grad_out_weight, grad_up, grad_down)
    shares = (
        lax.psum_scatter(grads[0], "seq", scatter_dimension=0, tiled=True),
        lax.psum_scatter(grads[1], "seq", scatter_dimension=0, tiled=True),
        lax.psum_scatter(grads[2], "seq", scatter_dimension=0, tiled=True),
        lax.psum_scatter(grads[3], "seq", scatter_dimension=0, tiled=True),
        lax.psum_scatter(grads[4], "seq", scatter_dimension=0, tiled=True),
        lax.psum_scatter(grads[5], "seq", scatter_dimension=0, tiled=True),
    )
    owned = lax.psum((shares[0], shares[1], shares[2], shares[3], shares[4], shares[5]), "grp")
    return (
        layer_out,
        grad_tokens,
        owned[0],
        owned[1],
        owned[2],
        owned[3],
        owned[4],
        owned[5],
        small[0],
        small[1],
        small[2],
        small[3],
        small[4],
    )


def solution(mesh):
    return jax.shard_map(
        shards,
        mesh=mesh,
        in_specs=(
            P("grp", "seq", None),
            P("grp"),
            P(("grp", "seq"), None),
            P(("grp", "seq"), None),
            P(("grp", "seq"), None),
            P(("grp", "seq"), None),
            P(("grp", "seq"), None),
            P(("grp", "seq"), None),
            P(("grp", "seq")),
            P(("grp", "seq")),
            P(("grp", "seq")),
            P(("grp", "seq")),
            P(),
            P("grp", "seq", None),
        ),
        out_specs=(
            P("grp", "seq", None),
            P("grp", "seq", None),
            P("seq", None),
            P("seq", None),
            P("seq", None),
            P("seq", None),
            P("seq", None),
            P("seq", None),
            P(),
            P(),
            P(),
            P(),
            P(),
        ),
        check_vma=False,
    )
```

profile of v0, /device:TPU:9, one launch (start us, length us, event | category | flops | bytes accessed | tf_op | source)
XLA Modules:
  0.0 1472.3 jit_solution(3057315746491439868)
XLA Ops:
  12.9 40.3 %all-reduce.6 = (bf16[1280]{0:T(1024)(128)(2,1)S(1)}, bf16[1280]{0:T(1024)(128)(2,1)}, bf16[1280]{0:T(1024)(128)(2,1)S(1)}, bf16[1280]{0:T(1024)(128)(2,1)S(1)}) all-reduce(bf16[1280]{0:T(1024)(128)(2,1)S(1)} %dynamic-update-slice, bf16[1280]{0:T(1024)(128)(2,1)S(1)} %dynamic-update-slice.3, ...), channel_id=1, replica_groups=mesh['grp'=4,'seq'=8] {'grp','seq'}, use_global_device_ids=true, to_apply=%add | all-reduce | flops 5120 | bytes 20480
  54.9 16.3 %all-gather.11.cloned.1.call-done = bf16[1280,1280]{1,0:T(8,128)(2,1)} async-done(((bf16[40,1280]{1,0:T(8,128)(2,1)}), bf16[1280,1280]{1,0:T(8,128)(2,1)}) %all-gather.11.cloned.1.call-update) | async-done | bytes 3276816 | tf_op jit(solution)/shard_map/all_gather | solution.py:81
  71.2 3.4 fusion.102
  74.6 57.6 %all-gather.17.cloned.1.call-done = bf16[1280,1280]{1,0:T(8,128)(2,1)} async-done(((bf16[40,1280]{1,0:T(8,128)(2,1)}), bf16[1280,1280]{1,0:T(8,128)(2,1)}) %all-gather.17.cloned.1.call-update) | async-done | bytes 3276816 | tf_op jit(solution)/shard_map/all_gather | solution.py:82
  132.3 3.3 fusion.105
  137.9 55.6 %all-gather.15.cloned.1.call-done = bf16[1280,1280]{1,0:T(8,128)(2,1)} async-done(((bf16[40,1280]{1,0:T(8,128)(2,1)}), bf16[1280,1280]{1,0:T(8,128)(2,1)}) %all-gather.15.cloned.1.call-update) | async-done | bytes 3276816 | tf_op jit(solution)/shard_map/all_gather | solution.py:80
  193.4 3.3 multiply_convert_fusion.3
  202.1 46.6 %all-gather.13.cloned.1.call-done = bf16[2,512,1280]{2,1,0:T(8,128)(2,1)} async-done(((bf16[2,64,1280]{2,1,0:T(8,128)(2,1)}), bf16[2,512,1280]{2,1,0:T(8,128)(2,1)}) %all-gather.13.cloned.1.call-update) | async-done | bytes 2621456 | tf_op jit(solution)/shard_map/all_gather | solution.py:158
  248.7 7.8 conditional.4
  250.1 3.0 copy.55
  259.4 45.2 %all-gather.19.cloned.1.call-done = bf16[2,512,1280]{2,1,0:T(8,128)(2,1)} async-done(((bf16[2,64,1280]{2,1,0:T(8,128)(2,1)}), bf16[2,512,1280]{2,1,0:T(8,128)(2,1)}) %all-gather.19.cloned.1.call-update) | async-done | bytes 2621456 | tf_op jit(solution)/shard_map/all_gather | solution.py:159
  304.7 22.5 %conditional.5 = (f32[2,64,16,80]{3,1,2,0:T(8,128)S(1)}, f32[2,64,16,80]{3,1,2,0:T(8,128)}) conditional(s32[]{:T(128)} %convert_element_type.144, f32[2,64,16,80]{3,1,2,0:T(8,128)S(1)} %broadcast_in_dim.135, (s32[64]{0:T(128)}, s32[2]{0:T(128)}, bf16[2,512,1280]{2,1,0:T(8,128)(2,1)}, bf16[2,64,16,80]{3,1,2,0:T(8,128)(2,1)S(1)}, ...), branch_computations={%region_6.7_spmd, %region_7.8_spmd} | conditional | flops 515277824 | bytes 61442444 | solution.py:152
  304.8 4.4 copy.60
  309.2 4.4 copy.58
  313.6 4.4 fusion.135
  319.8 4.2 fusion.13
  324.8 2.4 fusion.16
  328.3 37.9 %all-gather.21.cloned.1.call-done = bf16[1280,1280]{1,0:T(8,128)(2,1)} async-done(((bf16[40,1280]{1,0:T(8,128)(2,1)}), bf16[1280,1280]{1,0:T(8,128)(2,1)}) %all-gather.21.cloned.1.call-update) | async-done | bytes 3276816 | tf_op jit(solution)/shard_map/all_gather | solution.py:83
  366.2 2.6 multiply_reduce_fusion.3
  368.8 58.4 %all-gather.23.cloned.1.call-done = bf16[1280,1280]{1,0:T(8,128)(2,1)} async-done(((bf16[40,1280]{1,0:T(8,128)(2,1)}), bf16[1280,1280]{1,0:T(8,128)(2,1)}) %all-gather.23.cloned.1.call-update) | async-done | bytes 3276816 | tf_op jit(solution)/shard_map/all_gather | solution.py:84
  427.3 2.6 fusion.81
  429.9 58.5 %all-gather.25.cloned.1.call-done = bf16[1280,1280]{1,0:T(8,128)(2,1)} async-done(((bf16[40,1280]{1,0:T(8,128)(2,1)}), bf16[1280,1280]{1,0:T(8,128)(2,1)}) %all-gather.25.cloned.1.call-update) | async-done | bytes 3276816 | tf_op jit(solution)/shard_map/all_gather | solution.py:85
  488.4 4.0 convert_reduce_fusion.1
  492.5 1.9 multiply_reduce_fusion.1
  495.2 1.9 fusion.108
  497.2 2.6 reshape.441
  501.0 2.8 multiply_reduce_fusion
  505.1 25.3 %conditional.6 = (f32[2,64,16,80]{3,1,2,0:T(8,128)}) conditional(s32[]{:T(128)} %convert_element_type.144, f32[2,64,16,80]{3,1,2,0:T(8,128)S(1)} %broadcast_in_dim.135, (s32[64]{0:T(128)}, s32[2]{0:T(128)}, bf16[2,512,1280]{2,1,0:T(8,128)(2,1)}, bf16[2,64,16,80]{3,1,2,0:T(8,128)(2,1)S(1)}, f32[2,16,64]{1,0,2:T(2,128)}, ...), branch_computations={%region_10.11_spmd, %region_11.12_spmd} | conditional | flops 509871104 | bytes 30263596 | solution.py:245
  505.1 4.4 copy.62
  509.5 4.4 fusion.136
  514.0 4.5 copy.64
  518.4 1.5 copy.66
  520.0 1.5 copy.63
  523.6 6.9 fusion.21
  530.5 2.5 fusion.112
  534.1 1.6 reshape.442
  535.7 4.5 convolution_bitcast_fusion.7
  540.5 3.9 convolution_bitcast_fusion.4
  545.3 3.8 convolution_bitcast_fusion.3
  550.1 4.9 convolution_bitcast_fusion.2
  555.8 27.4 %all_gather.72 = f32[2,16,512]{1,0,2:T(2,128)} all-gather(f32[2,16,64]{1,0,2:T(2,128)} %add.232), channel_id=1, replica_groups=mesh['grp'=4,'seq'=8] {'seq'}, dimensions={2}, use_global_device_ids=true | all-gather | bytes 73728 | tf_op jit(solution)/shard_map/all_gather | solution.py:219
  583.1 28.7 %all_gather.74 = f32[2,16,512]{1,0,2:T(2,128)} all-gather(f32[2,16,64]{1,0,2:T(2,128)S(1)} %copy-done.22), channel_id=1, replica_groups=mesh['grp'=4,'seq'=8] {'seq'}, dimensions={2}, use_global_device_ids=true | all-gather | bytes 73728 | tf_op jit(solution)/shard_map/all_gather | solution.py:220
  611.9 32.8 %conditional.7 = (f32[2,64,16,80]{3,1,2,0:T(8,128)}, f32[2,64,16,80]{3,1,2,0:T(8,128)S(1)}) conditional(s32[]{:T(128)} %convert_element_type.165, f32[2,64,16,80]{3,1,2,0:T(8,128)S(1)} %broadcast_in_dim.135, (s32[64]{0:T(128)}, s32[2]{0:T(128)S(1)}, bf16[2,512,1280]{2,1,0:T(8,128)(2,1)}, bf16[2,64,1280]{2,1,0:T(8,128)(2,1)S(1)}, ...), branch_computations={%region_12.13_spmd, %region_13.14_spmd} | conditional | flops 682000512 | bytes 40436560 | solution.py:291
  611.9 4.4 copy.68
  616.4 1.6 reshape.434
  617.9 4.8 fusion.42
  622.7 4.5 copy.70
  631.7 1.6 reshape.436
  633.3 7.0 fusion.36
  640.3 4.4 fusion.37
  647.2 1.6 convert_element_type.168
  648.8 3.8 convolution_bitcast_fusion.6
  653.9 3.8 convolution_bitcast_fusion.5
  657.8 74.6 %reduce-scatter.7.cloned.1.call-done = f32[160,1280]{1,0:T(8,128)} async-done(((f32[1280,1280]{1,0:T(8,128)}), f32[160,1280]{1,0:T(8,128)}) %reduce-scatter.7.cloned.1.call-update) | async-done | bytes 819216 | tf_op jit(solution)/shard_map/reduce_scatter | solution.py:340
  732.4 124.7 %reduce-scatter.13.cloned.1.call-done = f32[160,1280]{1,0:T(8,128)} async-done(((f32[1280,1280]{1,0:T(8,128)}), f32[160,1280]{1,0:T(8,128)}) %reduce-scatter.13.cloned.1.call-update) | async-done | bytes 819216 | tf_op jit(solution)/shard_map/reduce_scatter | solution.py:343
  857.1 124.5 %reduce-scatter.15.cloned.1.call-done = f32[160,1280]{1,0:T(8,128)} async-done(((f32[1280,1280]{1,0:T(8,128)}), f32[160,1280]{1,0:T(8,128)}) %reduce-scatter.15.cloned.1.call-update) | async-done | bytes 819216 | tf_op jit(solution)/shard_map/reduce_scatter | solution.py:344
  981.6 124.7 %reduce-scatter.17.cloned.1.call-done = f32[160,1280]{1,0:T(8,128)} async-done(((f32[1280,1280]{1,0:T(8,128)}), f32[160,1280]{1,0:T(8,128)}) %reduce-scatter.17.cloned.1.call-update) | async-done | bytes 819216 | tf_op jit(solution)/shard_map/reduce_scatter | solution.py:345
  1106.3 124.3 %reduce-scatter.9.cloned.1.call-done = f32[160,1280]{1,0:T(8,128)} async-done(((f32[1280,1280]{1,0:T(8,128)}), f32[160,1280]{1,0:T(8,128)}) %reduce-scatter.9.cloned.1.call-update) | async-done | bytes 819216 | tf_op jit(solution)/shard_map/reduce_scatter | solution.py:341
  1230.6 124.7 %reduce-scatter.11.cloned.1.call-done = f32[160,1280]{1,0:T(8,128)} async-done(((f32[1280,1280]{1,0:T(8,128)}), f32[160,1280]{1,0:T(8,128)}) %reduce-scatter.11.cloned.1.call-update) | async-done | bytes 819216 | tf_op jit(solution)/shard_map/reduce_scatter | solution.py:342
  1355.4 3.3 fusion.64
  1364.0 42.6 %all-reduce.4 = (f32[1280]{0:T(1024)}, f32[1280]{0:T(1024)}, f32[1280]{0:T(1024)}, f32[1280]{0:T(1024)}, f32[80]{0:T(128)}) all-reduce(f32[1280]{0:T(1024)S(1)} %get-tuple-element.437, f32[1280]{0:T(1024)S(1)} %copy-done.34, f32[1280]{0:T(1024)S(1)} %copy-done.36, ...), channel_id=1, replica_groups=mesh['grp'=4,'seq'=8] {'grp','seq'}, use_global_device_ids=true, to_apply=%region_28.29 | all-reduce | flops 5200 | bytes 41600 | tf_op jit(solution)/shard_map/psum | solution.py:335
  1407.7 49.7 %all-reduce.9.cloned.1.call-done = (f32[160,1280]{1,0:T(8,128)}, f32[160,1280]{1,0:T(8,128)}, f32[160,1280]{1,0:T(8,128)}, f32[160,1280]{1,0:T(8,128)}, f32[160,1280]{1,0:T(8,128)}, /*index=5*/f32[160,1280]{1,0:T(8,128)}) async-done(((f32[160,1280]{1,0:T(8,128)}, f32[160,1280]{1,0:T(8,128)}, f32[160,1280]{1,0:T(8,128)}, f32[160,1280]{1,0:T(8,128)}, f32[160,1280]{1,0:T(8,128)}, ...) | async-done | bytes 4915216 | tf_op jit(solution)/shard_map/psum | solution.py:347
  1457.4 2.2 copy.117
  1459.6 2.2 copy.118
  (207 shorter events, 52.7 us)
Async XLA Ops:
  7.2 125.1 %copy-start = (bf16[2,64,1280]{2,1,0:T(8,128)(2,1)S(1)}, bf16[2,64,1280]{2,1,0:T(8,128)(2,1)}, u32[]{:S(2)}) copy-start(bf16[2,64,1280]{2,1,0:T(8,128)(2,1)} %param.22) | copy-start | bytes 983044
  7.2 64.0 %all-gather.11.cloned.1.call-start = ((), (), s32[]{:S(2)}) async-start(), calls=%async_computation.6 | async-start | bytes 3379200 | tf_op jit(solution)/shard_map/all_gather | solution.py:81
  7.9 124.4 %all-gather.17.cloned.1.call-start = ((), (), s32[]{:S(2)}) async-start(), calls=%async_computation.9 | async-start | bytes 3379200 | tf_op jit(solution)/shard_map/all_gather | solution.py:82
  8.7 184.7 %all-gather.15.cloned.1.call-start = ((), (), s32[]{:S(2)}) async-start(), calls=%async_computation.8 | async-start | bytes 3379200 | tf_op jit(solution)/shard_map/all_gather | solution.py:80
  9.4 239.3 %all-gather.13.cloned.1.call-start = ((), (), s32[]{:S(2)}) async-start(), calls=%async_computation.7 | async-start | bytes 2949120 | tf_op jit(solution)/shard_map/all_gather | solution.py:158
  54.9 138.6 %copy-start.28 = (f32[2,64]{1,0:T(2,128)}, f32[2,64]{1,0:T(2,128)S(1)}, u32[]{:S(2)}) copy-start(f32[2,64]{1,0:T(2,128)S(1)} %get-tuple-element.461) | copy-start | bytes 1540
  74.6 63.2 %copy-start.47 = (f32[80]{0:T(128)S(1)}, f32[80]{0:T(128)}, u32[]{:S(2)}) copy-start(f32[80]{0:T(128)} %param.34) | copy-start | bytes 964
  74.6 230.0 %all-gather.19.cloned.1.call-start = ((), (), s32[]{:S(2)}) async-start(), calls=%async_computation.10 | async-start | bytes 2949120 | tf_op jit(solution)/shard_map/all_gather | solution.py:159
  135.6 230.6 %all-gather.21.cloned.1.call-start = ((), (), s32[]{:S(2)}) async-start(), calls=%async_computation.11 | async-start | bytes 3379200 | tf_op jit(solution)/shard_map/all_gather | solution.py:83
  136.2 291.1 %all-gather.23.cloned.1.call-start = ((), (), s32[]{:S(2)}) async-start(), calls=%async_computation.12 | async-start | bytes 3379200 | tf_op jit(solution)/shard_map/all_gather | solution.py:84
  136.9 59.9 %copy-start.38 = (s32[2]{0:T(128)S(1)}, s32[2]{0:T(128)}, u32[]{:S(2)}) copy-start(s32[2]{0:T(128)} %param.23) | copy-start | bytes 28
  136.9 351.5 %all-gather.25.cloned.1.call-start = ((), (), s32[]{:S(2)}) async-start(), calls=%async_computation.13 | async-start | bytes 3379200 | tf_op jit(solution)/shard_map/all_gather | solution.py:85
  137.7 474.2 %all-gather.27.cloned.1.call-start = ((), (), s32[]{:S(2)}) async-start(), calls=%async_computation.14 | async-start | bytes 2949120 | tf_op jit(solution)/shard_map/all_gather | solution.py:296
  137.8 63.9 %copy-start.37 = (f32[80]{0:T(128)}, f32[80]{0:T(128)S(1)}, u32[]{:S(2)}) copy-start(f32[80]{0:T(128)S(1)} %fusion.126) | copy-start | bytes 964
  196.7 415.2 %all-gather.29.cloned.1.call-start = ((), (), s32[]{:S(2)}) async-start(), calls=%async_computation.15 | async-start | bytes 2949120 | tf_op jit(solution)/shard_map/all_gather | solution.py:297
  201.7 47.0 %copy-start.5 = (f32[2,64,16,80]{3,2,1,0:T(8,128)}, f32[2,64,16,80]{3,2,1,0:T(8,128)S(1)}, u32[]{:S(2)}) copy-start(f32[2,64,16,80]{3,2,1,0:T(8,128)S(1)} %reshape.440) | copy-start | bytes 1966084
  202.1 102.7 %copy-start.7 = (bf16[2,64,16,80]{3,1,2,0:T(8,128)(2,1)}, bf16[2,64,16,80]{3,1,2,0:T(8,128)(2,1)S(1)}, u32[]{:S(2)}) copy-start(bf16[2,64,16,80]{3,1,2,0:T(8,128)(2,1)S(1)} %multiply_convert_fusion.2) | copy-start | bytes 983044
  253.1 0.8 copy-start.26
  313.6 5.3 copy-start.40
  319.7 4.3 copy-start.9
  319.7 5.0 copy-start.12
  327.3 41.5 %copy-start.6 = (f32[2,64,16,80]{3,1,2,0:T(8,128)}, f32[2,64,16,80]{3,1,2,0:T(8,128)S(1)}, u32[]{:S(2)}) copy-start(f32[2,64,16,80]{3,1,2,0:T(8,128)S(1)} %get-tuple-element.333) | copy-start | bytes 1966084
  327.7 99.5 %copy-start.33 = (f32[1280]{0:T(1024)S(1)}, f32[1280]{0:T(1024)}, u32[]{:S(2)}) copy-start(f32[1280]{0:T(1024)} %convert_element_type.154) | copy-start | bytes 15364
  368.8 119.6 %copy-start.44 = (pred[2,64]{1,0:T(4,128)(4,1)S(1)}, pred[2,64]{1,0:T(4,128)(4,1)}, u32[]{:S(2)}) copy-start(pred[2,64]{1,0:T(4,128)(4,1)} %broadcast_compare_fusion.1) | copy-start | bytes 388
  368.8 125.6 %copy-start.31 = (f32[2,64]{1,0:T(2,128)}, f32[2,64]{1,0:T(2,128)S(1)}, u32[]{:S(2)}) copy-start(f32[2,64]{1,0:T(2,128)S(1)} %get-tuple-element.463) | copy-start | bytes 1540
  429.9 62.6 %copy-start.20 = (f32[2,64,1280]{2,1,0:T(8,128)}, f32[2,64,1280]{2,1,0:T(8,128)S(1)}, u32[]{:S(2)}) copy-start(f32[2,64,1280]{2,1,0:T(8,128)S(1)} %fusion.81) | copy-start | bytes 1966084
  488.4 4.0 copy-start.4
  492.4 1.9 copy-start.14
  492.4 1.9 copy-start.23
  492.5 2.7 copy-start.3
  497.1 8.0 copy-start.8
  497.2 235.2 %reduce-scatter.7.cloned.1.call-start = ((), (), s32[]{:S(2)}) async-start(), calls=%async_computation.16 | async-start | bytes 7372800 | tf_op jit(solution)/shard_map/reduce_scatter | solution.py:340
  514.0 9.6 copy-start.13
  540.2 316.9 %reduce-scatter.13.cloned.1.call-start = ((), (), s32[]{:S(2)}) async-start(), calls=%async_computation.19 | async-start | bytes 7372800 | tf_op jit(solution)/shard_map/reduce_scatter | solution.py:343
  544.3 1.0 copy-start.15
  544.3 1.0 copy-start.32
  544.3 437.2 %reduce-scatter.15.cloned.1.call-start = ((), (), s32[]{:S(2)}) async-start(), calls=%async_computation.20 | async-start | bytes 7372800 | tf_op jit(solution)/shard_map/reduce_scatter | solution.py:344
  549.1 1.0 copy-start.24
  549.1 1.0 copy-start.45
  549.1 557.2 %reduce-scatter.17.cloned.1.call-start = ((), (), s32[]{:S(2)}) async-start(), calls=%async_computation.21 | async-start | bytes 7372800 | tf_op jit(solution)/shard_map/reduce_scatter | solution.py:345
  555.0 28.2 %copy-start.22 = (f32[2,16,64]{1,0,2:T(2,128)S(1)}, f32[2,16,64]{1,0,2:T(2,128)}, u32[]{:S(2)}) copy-start(f32[2,16,64]{1,0,2:T(2,128)} %copy.81) | copy-start | bytes 24580
  555.0 56.9 %copy-start.10 = (bf16[2,64,1280]{2,1,0:T(8,128)(2,1)S(1)}, bf16[2,64,1280]{2,1,0:T(8,128)(2,1)}, u32[]{:S(2)}) copy-start(bf16[2,64,1280]{2,1,0:T(8,128)(2,1)} %fusion.102) | copy-start | bytes 983044
  555.0 56.9 %copy-start.39 = (s32[2]{0:T(128)S(1)}, s32[2]{0:T(128)}, u32[]{:S(2)}) copy-start(s32[2]{0:T(128)} %param.23) | copy-start | bytes 28
  555.0 675.6 %reduce-scatter.9.cloned.1.call-start = ((), (), s32[]{:S(2)}) async-start(), calls=%async_computation.17 | async-start | bytes 7372800 | tf_op jit(solution)/shard_map/reduce_scatter | solution.py:341
  622.7 9.0 copy-start.11
  633.3 7.0 copy-start.30
  644.7 4.0 copy-start.29
  652.6 702.7 %reduce-scatter.11.cloned.1.call-start = ((), (), s32[]{:S(2)}) async-start(), calls=%async_computation.18 | async-start | bytes 7372800 | tf_op jit(solution)/shard_map/reduce_scatter | solution.py:342
  657.7 697.6 %copy-start.42 = (bf16[1280]{0:T(1024)(128)(2,1)S(1)}, bf16[1280]{0:T(1024)(128)(2,1)}, u32[]{:S(2)}) copy-start(bf16[1280]{0:T(1024)(128)(2,1)} %get-tuple-element.451) | copy-start | bytes 7684
  657.7 697.6 %copy-start.43 = (f32[80]{0:T(128)S(1)}, f32[80]{0:T(128)}, u32[]{:S(2)}) copy-start(f32[80]{0:T(128)} %get-tuple-element.456) | copy-start | bytes 964
  657.7 697.6 %copy-start.48 = (f32[80]{0:T(128)S(1)}, f32[80]{0:T(128)}, u32[]{:S(2)}) copy-start(f32[80]{0:T(128)} %param.34) | copy-start | bytes 964
  657.8 799.6 %all-reduce.9.cloned.1.call-start = ((), (), s32[]{:S(2)}) async-start(), calls=%async_computation.22 | async-start | bytes 9830400 | tf_op jit(solution)/shard_map/psum | solution.py:347
  1355.3 3.4 copy-start.21
  1355.3 3.4 copy-start.46
  1358.7 2.0 copy-start.1
  1360.7 1.9 copy-start.2
  1362.6 1.4 copy-start.34
  1362.6 1.4 copy-start.35
  1362.6 1.4 copy-start.36
  1362.7 44.0 %copy-start.41 = (f32[2,64]{1,0:T(2,128)S(1)}, f32[2,64]{1,0:T(2,128)}, u32[]{:S(2)}) copy-start(f32[2,64]{1,0:T(2,128)} %get-tuple-element.460) | copy-start | bytes 1540
  1457.4 4.4 copy-start.19
  1457.4 5.3 copy-start.18
  1457.4 6.2 copy-start.17
  1459.6 4.8 copy-start.16
  (2 other events, 1.2 us)
Sparse Core Ops, SparseCore 0:
  10.9 60.2 all-gather.10
  74.0 58.2 all-gather.16
  135.1 58.2 all-gather.14
  196.0 52.6 all-gather.12
  251.3 53.2 all-gather.18
  307.3 58.7 all-gather.20
  369.0 58.2 all-gather.22
  430.1 58.2 all-gather.24
  491.2 52.6 all-gather.26
  546.5 62.1 all-gather.28
  612.3 120.0 reduce-scatter.6
  736.3 120.7 reduce-scatter.12
  860.7 120.7 reduce-scatter.14
  985.5 120.7 reduce-scatter.16
  1109.7 120.7 reduce-scatter.8
  1234.5 120.7 reduce-scatter.10
  1357.9 99.4 all-reduce.8
where the time goes:
time: 1480 us; the launch traced here: 1470 us
  waiting for transfers between devices  1130 us (76%)
  blocking collectives  139 us (9%)
  matrix products  94.3 us (6%)
  local copies, waits for them, and re-layouts  69.9 us (5%)
  other arithmetic  23.9 us (2%)
  between operations  16.3 us (1%)
    reduce_scatter x1, waiting for transfers between devices, shards(): lax.psum_scatter(grads[3], 'seq', scatter_dimension=0, tiled=True)  125 us
    reduce_scatter x1, waiting for transfers between devices, shards(): lax.psum_scatter(grads[5], 'seq', scatter_dimension=0, tiled=True)  125 us
    reduce_scatter x1, waiting for transfers between devices, shards(): lax.psum_scatter(grads[2], 'seq', scatter_dimension=0, tiled=True)  125 us
    reduce_scatter x1, waiting for transfers between devices, shards(): lax.psum_scatter(grads[4], 'seq', scatter_dimension=0, tiled=True)  124 us
    reduce_scatter x1, waiting for transfers between devices, shards(): lax.psum_scatter(grads[1], 'seq', scatter_dimension=0, tiled=True)  124 us
    reduce_scatter x1, waiting for transfers between devices, shards(): lax.psum_scatter(grads[0], 'seq', scatter_dimension=0, tiled=True)  74.6 us
    all_gather x1, waiting for transfers between devices, shards(): lax.all_gather(params[5], ('grp', 'seq'), axis=0, tiled=True)  58.5 us
    all_gather x1, waiting for transfers between devices, shards(): lax.all_gather(params[4], ('grp', 'seq'), axis=0, tiled=True)  58.4 us
  transfers between devices with their start and end apart: 17, of which 15 were waited for; matrix products, arithmetic and copies ran while one was open for 12% of the time, Pallas kernels for 0%

commit v1 on v0

--- a/solution.py
+++ b/solution.py
@@ -362,9 +362,228 @@
     )
 
 
+def swap(value, axis, bit, size):
+    return lax.ppermute(value, axis, [(i, i ^ bit) for i in range(size)])
+
+
+def in_order(pieces, index):
+    low, high = (index & 1) == 1, (index & 2) == 2
+    half = [jnp.where(low, pieces[p ^ 1], pieces[p]) for p in range(4)]
+    return [jnp.where(high, half[p ^ 2], half[p]) for p in range(4)]
+
+
+def pick(array, index, axis):
+    return lax.dynamic_index_in_dim(array, index, axis, keepdims=False)
+
+
+def gather_grp(value, g):
+    far = swap(value, "grp", 2, 4)
+    return in_order([value, swap(value, "grp", 1, 4), far, swap(far, "grp", 1, 4)], g)
+
+
+def gather_seq(value, z, y):
+    mine = jnp.stack(in_order([value] + [swap(value, "seq", 2 * k, 8) for k in (1, 2, 3)], z))
+    other = swap(mine, "seq", 1, 8)
+    return jnp.where(y == 0, jnp.stack([mine, other], 1), jnp.stack([other, mine], 1))
+
+
+def scatter_seq(keep, send, z):
+    total = keep.astype(jnp.float32) + swap(send, "seq", 1, 8).astype(jnp.float32)
+    low = total.astype(jnp.bfloat16)
+    own = pick(total, z, 0)
+    for k in (1, 2, 3):
+        own = own + swap(pick(low, z ^ k, 0), "seq", 2 * k, 8).astype(jnp.float32)
+    return own
+
+
+def quick(
+    tokens,
+    lengths,
+    query_weight,
+    key_weight,
+    value_weight,
+    out_weight,
+    up_weight,
+    down_weight,
+    norm_gain,
+    ff_gain,
+    up_bias,
+    down_bias,
+    query_scale,
+    cotangent,
+):
+    low, wide = jnp.bfloat16, jnp.float32
+    seq_count, rows, width = tokens.shape
+    head_size = query_scale.shape[0]
+    share = width // 8
+    own_heads = share // head_size
+    total_rows = 8 * rows
+    g, s = lax.axis_index("grp"), lax.axis_index("seq")
+    x, c, z, y = g // 2, g % 2, s // 2, s % 2
+    wrows = query_weight.shape[0]
+
+    def dot(a, b, dims):
+        return lax.dot_general(a, b, (dims, ((), ())), preferred_element_type=wide)
+
+    all_tokens = [gather_seq(tokens[i], z, y).reshape(total_rows, width) for i in range(seq_count)]
+    smalls = jnp.stack([norm_gain, ff_gain, up_bias, down_bias])
+    smalls = jnp.pad(smalls, ((0, 4), (0, 3 * share - wrows)))
+    payload = jnp.stack([w.reshape(wrows, 8, share) for w in (query_weight, key_weight, value_weight)], 2)
+    payload = payload.reshape(wrows, 8, 3 * share).transpose(1, 0, 2)
+    payload = jnp.concatenate([payload, jnp.broadcast_to(smalls, (8,) + smalls.shape)], 1)
+    columns = lax.all_to_all(payload, "seq", 0, 0, tiled=True)
+    columns = jnp.stack(gather_grp(columns, g))
+    w_qkv = columns[:, :, :wrows].reshape(width, 3 * share)
+    gains = columns[:, :, wrows : wrows + 4, :wrows].transpose(2, 0, 1, 3).reshape(4, width)
+    gain_one, gain_two, bias_up, bias_down = (gains[k].astype(wide) for k in range(4))
+
+    packed = jnp.stack([out_weight, up_weight, down_weight])
+    w_out, w_up, w_down = (
+        jnp.stack(gather_grp(gather_seq(w, z, y), g)).reshape(width, width)
+        for w in (out_weight, up_weight, down_weight)
+    )
+    factor = QCONST / math.sqrt(head_size)
+    scale = factor * jax.nn.softplus(query_scale)
+    scale_row = jnp.tile(scale, own_heads)
+
+    position = jnp.arange(total_rows, dtype=jnp.int32)
+    causal = position[None, :] <= position[:, None]
+
+    def split(a):
+        return a.reshape(total_rows, own_heads, head_size)
+
+    saved, mixed_parts = [], []
+    for i in range(seq_count):
+        tok = all_tokens[i].astype(wide)
+        inv = lax.rsqrt(jnp.mean(tok * tok, axis=-1, keepdims=True) + EPS)
+        normed = (tok * inv * gain_one).astype(low)
+        qkv = dot(normed, w_qkv, ((1,), (0,)))
+        query_raw = qkv[:, :share]
+        q = split((query_raw * scale_row).astype(low))
+        k = split(qkv[:, share : 2 * share].astype(low))
+        v = split(qkv[:, 2 * share :].astype(low))
+        allowed = causal & (position[None, :] < lengths[i])
+        scores = jnp.einsum("qhe,khe->hqk", q, k, preferred_element_type=wide)
+        scores = jnp.where(allowed, scores, NEG)
+        probs = jax.nn.softmax(scores, axis=-1)
+        att = jnp.einsum("hqk,khe->qhe", probs.astype(low), v, preferred_element_type=wide)
+        mixed_parts.append(att.astype(low).reshape(8, rows, share))
+        saved.append((tok * inv, normed, query_raw, q, k, v, probs))
+    att = lax.all_to_all(jnp.stack(mixed_parts, 1), "seq", 0, 0, tiled=True)
+    attended = att.reshape(8, seq_count * rows, share).transpose(1, 0, 2).reshape(-1, width)
+
+    inputs = tokens.reshape(-1, width).astype(wide)
+    hidden = inputs + dot(attended, w_out, ((1,), (0,)))
+    inv_two = lax.rsqrt(jnp.mean(hidden * hidden, axis=-1, keepdims=True) + EPS)
+    normed_two = (hidden * inv_two * gain_two).astype(low)
+    pre = dot(normed_two, w_up, ((1,), (0,))) + bias_up
+    sigma = jax.nn.sigmoid(pre)
+    act = (pre * sigma).astype(low)
+    layer_out = (hidden + dot(act, w_down, ((1,), (0,))) + bias_down).astype(low)
+    own_pos = s * rows + jnp.arange(rows, dtype=jnp.int32)
+    valid = own_pos[None, :] < lengths[:, None]
+    grad_out = jnp.where(valid[..., None], cotangent, jnp.zeros_like(cotangent)).reshape(-1, width)
+    grad_act = dot(grad_out, w_down, ((1,), (1,)))
+    grad_pre = (grad_act * sigma * (1.0 + pre * (1.0 - sigma))).astype(low)
+    grad_normed_two = dot(grad_pre, w_up, ((1,), (1,)))
+    grad_gain_two = jnp.sum(grad_normed_two * hidden * inv_two, axis=0)
+    weighted = grad_normed_two * gain_two
+    grad_hidden = (
+        grad_out.astype(wide)
+        + inv_two * weighted
+        - hidden * (inv_two * inv_two * inv_two) * jnp.mean(weighted * hidden, axis=-1, keepdims=True)
+    )
+    grad_mixed = grad_hidden.astype(low)
+    grad_att = dot(grad_mixed, w_out, ((1,), (1,))).astype(low)
+    grad_att = grad_att.reshape(seq_count * rows, 8, share).transpose(1, 0, 2)
+    grad_att = lax.all_to_all(grad_att, "seq", 0, 0, tiled=True).reshape(8, seq_count, rows, share)
+
+    left = jnp.concatenate([attended, normed_two, act], 1)
+    right = jnp.stack([grad_mixed, grad_pre, grad_out]).reshape(3, seq_count * rows, 2, width // 2)
+    left_two = jnp.concatenate([left, swap(left, "grp", 2, 4)], 0)
+    right_two = jnp.concatenate([pick(right, x, 2), swap(pick(right, 1 - x, 2), "grp", 2, 4)], 1)
+    right_two = right_two.reshape(3, 2 * seq_count * rows, 2, width // 4)
+    left_four = jnp.concatenate([left_two, swap(left_two, "grp", 1, 4)], 0)
+    right_four = jnp.concatenate([pick(right_two, c, 2), swap(pick(right_two, 1 - c, 2), "grp", 1, 4)], 1)
+    quarter = jnp.stack(
+        [dot(left_four[:, k * width : (k + 1) * width], right_four[k], ((0,), (0,))) for k in range(3)]
+    )
+    quarter = quarter.astype(low).reshape(3, 4, 2, share, width // 4).transpose(2, 1, 0, 3, 4)
+    ff_grads = scatter_seq(pick(quarter, y, 0), pick(quarter, 1 - y, 0), z).astype(low)
+    ff_grads = jnp.concatenate(gather_grp(ff_grads, g), 2).astype(wide)
+
+    grad_qkv_w = jnp.zeros((width, 3 * share), wide)
+    grad_gain_one = jnp.zeros((width,), wide)
+    grad_scale = jnp.zeros((head_size,), wide)
+    grad_normed = []
+    for i in range(seq_count):
+        unit, normed, query_raw, q, k, v, probs = saved[i]
+        ga = split(grad_att[:, i].reshape(total_rows, share))
+        grad_probs = jnp.einsum("qhe,khe->hqk", ga, v, preferred_element_type=wide)
+        delta = jnp.sum(grad_probs * probs, axis=-1, keepdims=True)
+        grad_scores = (probs * (grad_probs - delta)).astype(low)
+        gq = jnp.einsum("hqk,khe->qhe", grad_scores, k, preferred_element_type=wide).astype(low)
+        gk = jnp.einsum("hqk,qhe->khe", grad_scores, q, preferred_element_type=wide).astype(low)
+        gv = jnp.einsum("hqk,qhe->khe", probs.astype(low), ga, preferred_element_type=wide).astype(low)
+        gq_wide = gq.astype(wide)
+        grad_scale = grad_scale + jnp.sum(gq_wide * split(query_raw), axis=(0, 1))
+        gq = (gq_wide * scale).astype(low)
+        grads = jnp.concatenate([a.reshape(total_rows, share) for a in (gq, gk, gv)], 1)
+        grad_qkv_w = grad_qkv_w + dot(normed, grads, ((0,), (0,)))
+        partial = dot(grads, w_qkv, ((1,), (1,)))
+        grad_gain_one = grad_gain_one + jnp.sum(partial * unit, axis=0)
+        blocks = partial.astype(low).reshape(4, 2, rows, width)
+        grad_normed.append(scatter_seq(pick(blocks, y, 1), pick(blocks, 1 - y, 1), z))
+    grad_normed = jnp.concatenate(grad_normed, 0)
+    inv_one = lax.rsqrt(jnp.mean(inputs * inputs, axis=-1, keepdims=True) + EPS)
+    weighted = grad_normed * gain_one
+    grad_tokens = (
+        grad_hidden
+        + inv_one * weighted
+        - inputs * (inv_one * inv_one * inv_one) * jnp.mean(weighted * inputs, axis=-1, keepdims=True)
+    )
+
+    halves = grad_qkv_w.astype(low).reshape(8, 2, 2, wrows, 3 * share)
+    half = pick(halves, c, 2).astype(wide) + swap(pick(halves, 1 - c, 2), "grp", 1, 4).astype(wide)
+    half = half.astype(low)
+    part = pick(half, x, 1).astype(wide) + swap(pick(half, 1 - x, 1), "grp", 2, 4).astype(wide)
+    part = lax.all_to_all(part.astype(low), "seq", 0, 0, tiled=True)
+    qkv_grads = jnp.stack(gather_grp(part, g)).astype(wide).reshape(4, 8, wrows, 3, share)
+    qkv_grads = qkv_grads.transpose(3, 0, 2, 1, 4).reshape(3, share, width)
+
+    sums = jnp.stack(
+        [
+            grad_gain_one,
+            grad_gain_two,
+            jnp.sum(grad_pre.astype(wide), axis=0),
+            jnp.sum(grad_out.astype(wide), axis=0),
+            jnp.pad(grad_scale * factor * jax.nn.sigmoid(query_scale), (0, width - head_size)),
+        ]
+    )
+    for axis, bit, size in (("grp", 1, 4), ("grp", 2, 4), ("seq", 1, 8), ("seq", 2, 8), ("seq", 4, 8)):
+        sums = sums + swap(sums, axis, bit, size)
+    shape = (seq_count, rows, width)
+    return (
+        layer_out.reshape(shape),
+        grad_tokens.reshape(shape),
+        qkv_grads[0],
+        qkv_grads[1],
+        qkv_grads[2],
+        ff_grads[0],
+        ff_grads[1],
+        ff_grads[2],
+        sums[0],
+        sums[1],
+        sums[2],
+        sums[3],
+        sums[4, :head_size],
+    )
+
+
 def solution(mesh):
+    fits = mesh.shape["grp"] == 4 and mesh.shape["seq"] == 8
     return jax.shard_map(
-        shards,
+        quick if fits else shards,
         mesh=mesh,
         in_specs=(
             P("grp", "seq", None),

time: 1480 us -> 483 us (0.33)
  waiting for transfers between devices: 1130 us -> 188 us
  blocking collectives: 139 us -> 0 us
  starting transfers between devices: 1.15 us -> 103 us
  matrix products: 94.3 us -> 46.4 us
  other arithmetic: 23.9 us -> 53.9 us
    reduce_scatter x6 -> x0, waiting for transfers between devices: 697 us -> none  [the longest x1 125 us: shards(): lax.psum_scatter(grads[3], 'seq', scatter_dimension=0, tiled=True)]
    all_gather x10 -> x0, waiting for transfers between devices: 376 us -> none  [the longest x1 58.5 us: shards(): lax.all_gather(params[5], ('grp', 'seq'), axis=0, tiled=True)]
    ppermute x0 -> x61, waiting for transfers between devices: none -> 154 us  [swap(): return lax.ppermute(value, axis, [(i, i ^ bit) for i in range(size)])]
    ppermute x0 -> x61, starting transfers between devices: none -> 80.5 us  [swap(): return lax.ppermute(value, axis, [(i, i ^ bit) for i in range(size)])]
    all_gather x2 -> x0, blocking collectives: 56.1 us -> none  [the longest x1 28.7 us: shards(): lax.all_gather(delta, 'seq', axis=2, tiled=True)]
    dot_general x27 -> x25, matrix products: 94.3 us -> 41.8 us  [the longest x15 26.9 us: dot(): return lax.dot_general(a, b, (dims, ((), ())), preferred_element_type=wide)]
    psum x1 -> x0, waiting for transfers between devices: 49.7 us -> none  [shards(): lax.psum((shares[0], shares[1], shares[2], shares[3], shares[4], shares[5...]
    psum x1 -> x0, blocking collectives: 42.6 us -> none  [shards(): lax.psum((grad_gain_one, grad_gain_two, grad_bias_up, grad_bias_down, gra...]
  transfers between devices with their start and end apart: 17 -> 65, of which waited for: 15 -> 25; matrix products, arithmetic and copies ran while one was open for 12% -> 33% of each run, Pallas kernels for 0% -> 0%
where the time goes in v1:
time: 483 us; the launch traced here: 474 us
  waiting for transfers between devices  188 us (39%)
  starting transfers between devices  103 us (21%)
  local copies, waits for them, and re-layouts  79.7 us (17%)
  other arithmetic  53.9 us (11%)
  matrix products  46.4 us (10%)
    ppermute x61, waiting for transfers between devices, swap(): return lax.ppermute(value, axis, [(i, i ^ bit) for i in range(size)])  154 us
    ppermute x61, starting transfers between devices, swap(): return lax.ppermute(value, axis, [(i, i ^ bit) for i in range(size)])  80.5 us
    all_to_all x1, waiting for transfers between devices, quick(): part = lax.all_to_all(part.astype(low), 'seq', 0, 0, tiled=True)  26.9 us
    dot_general x15, matrix products, dot(): return lax.dot_general(a, b, (dims, ((), ())), preferred_element_type=wide)  26.9 us
  transfers between devices with their start and end apart: 65, of which 25 were waited for; matrix products, arithmetic and copies ran while one was open for 33% of the time, Pallas kernels for 0%

profile of v1, /device:TPU:9, one launch (start us, length us, event | category | flops | bytes accessed | tf_op | source)
XLA Modules:
  0.0 474.0 jit_solution(7434159121704183461)
XLA Ops:
  14.2 5.7 %all-to-all-start = ((bf16[8,48,480]{2,1,0:T(8,128)(2,1)}), bf16[8,48,480]{2,1,0:T(8,128)(2,1)}, u32[]{:S(2)}, u32[]{:S(2)}) async-start(bf16[8,48,480]{2,1,0:T(8,128)(2,1)} %copy.236), calls=%async_computation | async-start | bytes 786432 | tf_op jit(solution)/shard_map/all_to_all | solution.py:434
  24.2 2.3 collective-permute-start.11
  29.2 2.1 collective-permute-start.1
  31.5 2.6 collective-permute-done.11
  34.1 7.3 %collective-permute-done.12 = bf16[40,1280]{1,0:T(8,128)(2,1)S(1)} collective-permute-done((bf16[40,1280]{1,0:T(8,128)(2,1)S(1)}, bf16[40,1280]{1,0:T(8,128)(2,1)S(1)}, u32[]{:S(2)}, u32[]{:S(2)}) %collective-permute-start.12) | collective-permute-done | bytes 102432 | tf_op jit(solution)/shard_map/ppermute | solution.py:366
  41.4 3.3 collective-permute-start.8
  44.8 6.3 %collective-permute-done = bf16[64,1280]{1,0:T(8,128)(2,1)S(1)} collective-permute-done((bf16[64,1280]{1,0:T(8,128)(2,1)S(1)}, bf16[64,1280]{1,0:T(8,128)(2,1)S(1)}, u32[]{:S(2)}, u32[]{:S(2)}) %collective-permute-start) | collective-permute-done | bytes 163872 | tf_op jit(solution)/shard_map/ppermute | solution.py:366
  51.2 6.2 %collective-permute-done.1 = bf16[64,1280]{1,0:T(8,128)(2,1)S(1)} collective-permute-done((bf16[64,1280]{1,0:T(8,128)(2,1)S(1)}, bf16[64,1280]{1,0:T(8,128)(2,1)S(1)}, u32[]{:S(2)}, u32[]{:S(2)}) %collective-permute-start.1) | collective-permute-done | bytes 163872 | tf_op jit(solution)/shard_map/ppermute | solution.py:366
  58.8 4.1 collective-permute-done.7
  68.0 15.1 %collective-permute-done.14 = bf16[4,40,1280]{2,1,0:T(8,128)(2,1)S(1)} collective-permute-done((bf16[4,40,1280]{2,1,0:T(8,128)(2,1)S(1)}, bf16[4,40,1280]{2,1,0:T(8,128)(2,1)S(1)}, u32[]{:S(2)}, u32[]{:S(2)}) %collective-permute-start.14) | collective-permute-done | bytes 409632 | tf_op jit(solution)/shard_map/ppermute | solution.py:366
  89.1 22.2 %collective-permute-done.10 = bf16[4,64,1280]{2,1,0:T(8,128)(2,1)S(1)} collective-permute-done((bf16[4,64,1280]{2,1,0:T(8,128)(2,1)}, bf16[4,64,1280]{2,1,0:T(8,128)(2,1)S(1)}, u32[]{:S(2)}, u32[]{:S(2)}) %collective-permute-start.10) | collective-permute-done | bytes 655392 | tf_op jit(solution)/shard_map/ppermute | solution.py:366
  113.0 3.9 collective-permute-start.6
  116.9 22.8 %collective-permute-done.4 = bf16[8,48,480]{2,1,0:T(8,128)(2,1)S(1)} collective-permute-done((bf16[8,48,480]{2,1,0:T(8,128)(2,1)}, bf16[8,48,480]{2,1,0:T(8,128)(2,1)S(1)}, u32[]{:S(2)}, u32[]{:S(2)}) %collective-permute-start.4) | collective-permute-done | bytes 368672 | tf_op jit(solution)/shard_map/ppermute | solution.py:366
  139.7 7.8 %collective-permute-start.5 = (bf16[8,48,480]{2,1,0:T(8,128)(2,1)S(1)}, bf16[8,48,480]{2,1,0:T(8,128)(2,1)S(1)}, u32[]{:S(2)}, u32[]{:S(2)}) collective-permute-start(bf16[8,48,480]{2,1,0:T(8,128)(2,1)S(1)} %collective-permute-done.4), channel_id=1, source_target_pairs={{0,8},{8,0},{16,24},{24,16},{1,9},{9,1},{17,25},{25,17},{2,10},{10... | collective-permute-start | bytes 1105928 | tf_op jit(solution)/shard_map/ppermute | solution.py:366
  150.6 2.5 fusion.3
  155.9 2.3 fusion.124
  159.5 2.3 fusion.122
  164.8 7.2 %all-to-all-start.1 = ((bf16[8,2,64,160]{3,2,1,0:T(8,128)(2,1)}), bf16[8,2,64,160]{3,2,1,0:T(8,128)(2,1)}, u32[]{:S(2)}, u32[]{:S(2)}) async-start(bf16[8,2,64,160]{3,2,1,0:T(8,128)(2,1)} %copy.243), calls=%async_computation.1 | async-start | bytes 1048576 | tf_op jit(solution)/shard_map/all_to_all | solution.py:472
  176.1 7.3 %all-to-all-done.1 = bf16[8,2,64,160]{3,2,1,0:T(8,128)(2,1)} async-done(((bf16[8,2,64,160]{3,2,1,0:T(8,128)(2,1)}), bf16[8,2,64,160]{3,2,1,0:T(8,128)(2,1)}, u32[]{:S(2)}, u32[]{:S(2)}) %all-to-all-start.1) | async-done | bytes 327712 | tf_op jit(solution)/shard_map/all_to_all | solution.py:472
  183.4 2.0 copy.244
  187.2 3.2 collective-permute-start.24
  190.9 2.8 select_bitcast_fusion.11
  199.2 1.9 select_bitcast_fusion.3
  206.5 1.9 convolution_convert_fusion
  213.9 5.4 %all-to-all-start.2 = ((bf16[8,128,160]{1,2,0:T(8,128)(2,1)}), bf16[8,128,160]{1,2,0:T(8,128)(2,1)}, u32[]{:S(2)}, u32[]{:S(2)}) async-start(bf16[8,128,160]{1,2,0:T(8,128)(2,1)} %bitcast.423), calls=%async_computation.2 | async-start | bytes 655360 | tf_op jit(solution)/shard_map/all_to_all | solution.py:499
  223.0 3.0 constant_dynamic-slice_fusion
  230.3 3.0 copy.277
  233.5 3.4 fusion.7
  236.9 2.7 collective-permute-done.47
  239.6 2.0 copy.278
  241.6 2.2 fusion.40
  243.9 1.9 collective-permute-start.48
  245.8 2.0 copy.257
  251.6 3.1 convolution_convert_fusion.7
  254.7 2.3 multiply_reduce_fusion.5
  262.1 3.1 convolution_convert_fusion.4
  265.2 2.4 multiply_reduce_fusion.4
  270.3 2.8 multiply_reduce_fusion
  273.3 2.7 multiply_reduce_fusion.1
  276.2 2.3 fusion.59
  289.3 2.1 collective-permute-start.60
  296.7 4.5 collective-permute-start.46
  303.6 2.3 collective-permute-start.34
  306.0 8.9 %collective-permute-done.36 = bf16[4,64,1280]{2,1,0:T(8,128)(2,1)S(1)} collective-permute-done((bf16[4,64,1280]{2,1,0:T(8,128)(2,1)S(1)}, bf16[4,64,1280]{2,1,0:T(8,128)(2,1)S(1)}, u32[]{:S(2)}, u32[]{:S(2)}) %collective-permute-start.36) | collective-permute-done | bytes 655392 | tf_op jit(solution)/shard_map/ppermute | solution.py:366
  314.9 2.1 collective-permute-start.35
  318.6 3.3 collective-permute-done.35
  324.0 9.1 %collective-permute-done.38 = bf16[64,1280]{1,0:T(8,128)(2,1)S(1)} collective-permute-done((bf16[64,1280]{1,0:T(8,128)(2,1)S(1)}, bf16[64,1280]{1,0:T(8,128)(2,1)S(1)}, u32[]{:S(2)}, u32[]{:S(2)}) %collective-permute-start.38) | collective-permute-done | bytes 163872 | tf_op jit(solution)/shard_map/ppermute | solution.py:366
  333.0 4.6 collective-permute-done.39
  338.4 6.0 %pad_maximum_fusion = bf16[512,3840]{1,0:T(8,128)(2,1)S(1)} fusion(bf16[256,3840]{1,0:T(8,128)(2,1)S(1)} %collective-permute-done.46, bf16[128,3840]{1,0:T(8,128)(2,1)} %collective-permute-done.45, bf16[128,1280]{1,0:T(8,128)(2,1)S(1)} %copy-done.11, bf16[128,1280]{1,0:T(8,128)(2,1)S(1)} %copy-done.16, bf16[128,1280]{1,0:T(8,128)(2,1)S(1)} %copy-done.13), kind=kLoop, calls=%fused_computation.3 | loop fusion | flops 19660800 | bytes 7864320 | tf_op jit(solution)/shard_map/concatenate | solution.py:506
  361.2 4.2 all-to-all-start.3
  366.8 26.9 %all-to-all-done.3 = bf16[8,40,480]{2,1,0:T(8,128)(2,1)} async-done(((bf16[8,40,480]{2,1,0:T(8,128)(2,1)}), bf16[8,40,480]{2,1,0:T(8,128)(2,1)}, u32[]{:S(2)}, u32[]{:S(2)}) %all-to-all-start.3) | async-done | bytes 307232 | tf_op jit(solution)/shard_map/all_to_all | solution.py:550
  394.2 3.3 collective-permute-start.44
  397.5 2.5 collective-permute-done.42
  400.0 4.2 collective-permute-start.43
  404.2 3.4 fusion.110
  408.6 2.2 collective-permute-start.51
  416.6 7.9 %collective-permute-done.50 = bf16[3,160,320]{2,1,0:T(8,128)(2,1)S(1)} collective-permute-done((bf16[3,160,320]{2,1,0:T(8,128)(2,1)}, bf16[3,160,320]{2,1,0:T(8,128)(2,1)S(1)}, u32[]{:S(2)}, u32[]{:S(2)}) %collective-permute-start.50) | collective-permute-done | bytes 307232 | tf_op jit(solution)/shard_map/ppermute | solution.py:366
  424.5 3.3 collective-permute-done.51
  427.8 16.0 %collective-permute-done.52 = bf16[3,160,320]{2,1,0:T(8,128)(2,1)} collective-permute-done((bf16[3,160,320]{2,1,0:T(8,128)(2,1)S(1)}, bf16[3,160,320]{2,1,0:T(8,128)(2,1)}, u32[]{:S(2)}, u32[]{:S(2)}) %collective-permute-start.52) | collective-permute-done | bytes 307232 | tf_op jit(solution)/shard_map/ppermute | solution.py:366
  443.8 2.3 fusion.29
  446.3 2.3 convert_bitcast_fusion
  450.1 5.2 %collective-permute-done.53 = bf16[3,160,320]{2,1,0:T(8,128)(2,1)} collective-permute-done((bf16[3,160,320]{2,1,0:T(8,128)(2,1)}, bf16[3,160,320]{2,1,0:T(8,128)(2,1)}, u32[]{:S(2)}, u32[]{:S(2)}) %collective-permute-start.53) | collective-permute-done | bytes 307232 | tf_op jit(solution)/shard_map/ppermute | solution.py:366
  455.3 2.0 collective-permute-start.54
  457.3 4.2 fusion.114
  (421 shorter events, 149.3 us)
Async XLA Ops:
  0.7 22.9 %collective-permute-start.18 = (bf16[40,1280]{1,0:T(8,128)(2,1)}, bf16[40,1280]{1,0:T(8,128)(2,1)S(1)}, u32[]{:S(2)}, u32[]{:S(2)}) collective-permute-start(bf16[40,1280]{1,0:T(8,128)(2,1)} %param.20), channel_id=1, source_target_pairs={{0,6},{1,7},{2,4},{3,5},{4,2},{5,3},{6,0},{7,1},{8,14},{9,15},{10,... | collective-permute-start | bytes 307208 | tf_op jit(solution)/shard_map/ppermute | solution.py:366
  2.0 22.2 %collective-permute-start.19 = (bf16[40,1280]{1,0:T(8,128)(2,1)}, bf16[40,1280]{1,0:T(8,128)(2,1)S(1)}, u32[]{:S(2)}, u32[]{:S(2)}) collective-permute-start(bf16[40,1280]{1,0:T(8,128)(2,1)} %param.20), channel_id=1, source_target_pairs={{0,4},{1,5},{2,6},{3,7},{4,0},{5,1},{6,2},{7,3},{8,12},{9,13},{10,... | collective-permute-start | bytes 307208 | tf_op jit(solution)/shard_map/ppermute | solution.py:366
  3.1 23.4 %collective-permute-start.20 = (bf16[40,1280]{1,0:T(8,128)(2,1)}, bf16[40,1280]{1,0:T(8,128)(2,1)S(1)}, u32[]{:S(2)}, u32[]{:S(2)}) collective-permute-start(bf16[40,1280]{1,0:T(8,128)(2,1)} %param.20), channel_id=1, source_target_pairs={{0,2},{1,3},{2,0},{3,1},{4,6},{5,7},{6,4},{7,5},{8,10},{9,11},{10,... | collective-permute-start | bytes 307208 | tf_op jit(solution)/shard_map/ppermute | solution.py:366
  4.2 23.5 %collective-permute-start.25 = (bf16[40,1280]{1,0:T(8,128)(2,1)}, bf16[40,1280]{1,0:T(8,128)(2,1)S(1)}, u32[]{:S(2)}, u32[]{:S(2)}) collective-permute-start(bf16[40,1280]{1,0:T(8,128)(2,1)} %param.21), channel_id=1, source_target_pairs={{0,6},{1,7},{2,4},{3,5},{4,2},{5,3},{6,0},{7,1},{8,14},{9,15},{10,... | collective-permute-start | bytes 307208 | tf_op jit(solution)/shard_map/ppermute | solution.py:366
  5.4 22.4 %collective-permute-start.26 = (bf16[40,1280]{1,0:T(8,128)(2,1)}, bf16[40,1280]{1,0:T(8,128)(2,1)S(1)}, u32[]{:S(2)}, u32[]{:S(2)}) collective-permute-start(bf16[40,1280]{1,0:T(8,128)(2,1)} %param.21), channel_id=1, source_target_pairs={{0,4},{1,5},{2,6},{3,7},{4,0},{5,1},{6,2},{7,3},{8,12},{9,13},{10,... | collective-permute-start | bytes 307208 | tf_op jit(solution)/shard_map/ppermute | solution.py:366
  14.2 74.9 %all-to-all-start = ((bf16[8,48,480]{2,1,0:T(8,128)(2,1)}), bf16[8,48,480]{2,1,0:T(8,128)(2,1)}, u32[]{:S(2)}, u32[]{:S(2)}) async-start(bf16[8,48,480]{2,1,0:T(8,128)(2,1)} %copy.236), calls=%async_computation | async-start | bytes 786432 | tf_op jit(solution)/shard_map/all_to_all | solution.py:434
  23.6 5.6 %collective-permute-start.27 = (bf16[40,1280]{1,0:T(8,128)(2,1)S(1)}, bf16[40,1280]{1,0:T(8,128)(2,1)S(1)}, u32[]{:S(2)}, u32[]{:S(2)}) collective-permute-start(bf16[40,1280]{1,0:T(8,128)(2,1)S(1)} %copy-done.65), channel_id=1, source_target_pairs={{0,2},{1,3},{2,0},{3,1},{4,6},{5,7},{6,4},{7,5},{8,10},{9,11},{10,... | collective-permute-start | bytes 307208 | tf_op jit(solution)/shard_map/ppermute | solution.py:366
  24.2 9.8 %collective-permute-start.11 = (bf16[40,1280]{1,0:T(8,128)(2,1)S(1)}, bf16[40,1280]{1,0:T(8,128)(2,1)S(1)}, u32[]{:S(2)}, u32[]{:S(2)}) collective-permute-start(bf16[40,1280]{1,0:T(8,128)(2,1)S(1)} %copy-done.67), channel_id=1, source_target_pairs={{0,6},{1,7},{2,4},{3,5},{4,2},{5,3},{6,0},{7,1},{8,14},{9,15},{10,... | collective-permute-start | bytes 307208 | tf_op jit(solution)/shard_map/ppermute | solution.py:366
  26.6 14.8 %collective-permute-start.12 = (bf16[40,1280]{1,0:T(8,128)(2,1)S(1)}, bf16[40,1280]{1,0:T(8,128)(2,1)S(1)}, u32[]{:S(2)}, u32[]{:S(2)}) collective-permute-start(bf16[40,1280]{1,0:T(8,128)(2,1)S(1)} %copy-done.67), channel_id=1, source_target_pairs={{0,4},{1,5},{2,6},{3,7},{4,0},{5,1},{6,2},{7,3},{8,12},{9,13},{10,... | collective-permute-start | bytes 307208 | tf_op jit(solution)/shard_map/ppermute | solution.py:366
  27.8 13.6 %collective-permute-start.13 = (bf16[40,1280]{1,0:T(8,128)(2,1)S(1)}, bf16[40,1280]{1,0:T(8,128)(2,1)S(1)}, u32[]{:S(2)}, u32[]{:S(2)}) collective-permute-start(bf16[40,1280]{1,0:T(8,128)(2,1)S(1)} %copy-done.67), channel_id=1, source_target_pairs={{0,2},{1,3},{2,0},{3,1},{4,6},{5,7},{6,4},{7,5},{8,10},{9,11},{10,... | collective-permute-start | bytes 307208 | tf_op jit(solution)/shard_map/ppermute | solution.py:366
  27.8 23.3 %collective-permute-start = (bf16[64,1280]{1,0:T(8,128)(2,1)S(1)}, bf16[64,1280]{1,0:T(8,128)(2,1)S(1)}, u32[]{:S(2)}, u32[]{:S(2)}) collective-permute-start(bf16[64,1280]{1,0:T(8,128)(2,1)S(1)} %get-tuple-element.137), channel_id=1, source_target_pairs={{0,6},{1,7},{2,4},{3,5},{4,2},{5,3},{6,0},{7,1},{8,14},{9,15},{10,... | collective-permute-start | bytes 491528 | tf_op jit(solution)/shard_map/ppermute | solution.py:366
  29.2 28.1 %collective-permute-start.1 = (bf16[64,1280]{1,0:T(8,128)(2,1)S(1)}, bf16[64,1280]{1,0:T(8,128)(2,1)S(1)}, u32[]{:S(2)}, u32[]{:S(2)}) collective-permute-start(bf16[64,1280]{1,0:T(8,128)(2,1)S(1)} %get-tuple-element.137), channel_id=1, source_target_pairs={{0,4},{1,5},{2,6},{3,7},{4,0},{5,1},{6,2},{7,3},{8,12},{9,13},{10,... | collective-permute-start | bytes 491528 | tf_op jit(solution)/shard_map/ppermute | solution.py:366
  34.1 24.7 %collective-permute-start.2 = (bf16[64,1280]{1,0:T(8,128)(2,1)S(1)}, bf16[64,1280]{1,0:T(8,128)(2,1)S(1)}, u32[]{:S(2)}, u32[]{:S(2)}) collective-permute-start(bf16[64,1280]{1,0:T(8,128)(2,1)S(1)} %get-tuple-element.137), channel_id=1, source_target_pairs={{0,2},{1,3},{2,0},{3,1},{4,6},{5,7},{6,4},{7,5},{8,10},{9,11},{10,... | collective-permute-start | bytes 491528 | tf_op jit(solution)/shard_map/ppermute | solution.py:366
  41.4 21.5 %collective-permute-start.7 = (bf16[64,1280]{1,0:T(8,128)(2,1)S(1)}, bf16[64,1280]{1,0:T(8,128)(2,1)S(1)}, u32[]{:S(2)}, u32[]{:S(2)}) collective-permute-start(bf16[64,1280]{1,0:T(8,128)(2,1)S(1)} %get-tuple-element.138), channel_id=1, source_target_pairs={{0,6},{1,7},{2,4},{3,5},{4,2},{5,3},{6,0},{7,1},{8,14},{9,15},{10,... | collective-permute-start | bytes 491528 | tf_op jit(solution)/shard_map/ppermute | solution.py:366
  41.4 23.1 %collective-permute-start.8 = (bf16[64,1280]{1,0:T(8,128)(2,1)S(1)}, bf16[64,1280]{1,0:T(8,128)(2,1)S(1)}, u32[]{:S(2)}, u32[]{:S(2)}) collective-permute-start(bf16[64,1280]{1,0:T(8,128)(2,1)S(1)} %get-tuple-element.138), channel_id=1, source_target_pairs={{0,4},{1,5},{2,6},{3,7},{4,0},{5,1},{6,2},{7,3},{8,12},{9,13},{10,... | collective-permute-start | bytes 491528 | tf_op jit(solution)/shard_map/ppermute | solution.py:366
  51.1 13.4 %collective-permute-start.9 = (bf16[64,1280]{1,0:T(8,128)(2,1)S(1)}, bf16[64,1280]{1,0:T(8,128)(2,1)S(1)}, u32[]{:S(2)}, u32[]{:S(2)}) collective-permute-start(bf16[64,1280]{1,0:T(8,128)(2,1)S(1)} %get-tuple-element.138), channel_id=1, source_target_pairs={{0,2},{1,3},{2,0},{3,1},{4,6},{5,7},{6,4},{7,5},{8,10},{9,11},{10,... | collective-permute-start | bytes 491528 | tf_op jit(solution)/shard_map/ppermute | solution.py:366
  57.4 27.2 %collective-permute-start.28 = (bf16[4,40,1280]{2,1,0:T(8,128)(2,1)S(1)}, bf16[4,40,1280]{2,1,0:T(8,128)(2,1)S(1)}, u32[]{:S(2)}, u32[]{:S(2)}) collective-permute-start(bf16[4,40,1280]{2,1,0:T(8,128)(2,1)S(1)} %get-tuple-element.111), channel_id=1, source_target_pairs={{0,1},{1,0},{2,3},{3,2},{4,5},{5,4},{6,7},{7,6},{8,9},{9,8},{10,11... | collective-permute-start | bytes 1228808 | tf_op jit(solution)/shard_map/ppermute | solution.py:366
  58.8 28.3 %collective-permute-start.21 = (bf16[4,40,1280]{2,1,0:T(8,128)(2,1)S(1)}, bf16[4,40,1280]{2,1,0:T(8,128)(2,1)S(1)}, u32[]{:S(2)}, u32[]{:S(2)}) collective-permute-start(bf16[4,40,1280]{2,1,0:T(8,128)(2,1)S(1)} %get-tuple-element.118), channel_id=1, source_target_pairs={{0,1},{1,0},{2,3},{3,2},{4,5},{5,4},{6,7},{7,6},{8,9},{9,8},{10,11... | collective-permute-start | bytes 1228808 | tf_op jit(solution)/shard_map/ppermute | solution.py:366
  62.9 20.2 %collective-permute-start.14 = (bf16[4,40,1280]{2,1,0:T(8,128)(2,1)S(1)}, bf16[4,40,1280]{2,1,0:T(8,128)(2,1)S(1)}, u32[]{:S(2)}, u32[]{:S(2)}) collective-permute-start(bf16[4,40,1280]{2,1,0:T(8,128)(2,1)S(1)} %get-tuple-element.124), channel_id=1, source_target_pairs={{0,1},{1,0},{2,3},{3,2},{4,5},{5,4},{6,7},{7,6},{8,9},{9,8},{10,11... | collective-permute-start | bytes 1228808 | tf_op jit(solution)/shard_map/ppermute | solution.py:366
  65.6 47.4 %collective-permute-start.3 = (bf16[4,64,1280]{2,1,0:T(8,128)(2,1)}, bf16[4,64,1280]{2,1,0:T(8,128)(2,1)S(1)}, u32[]{:S(2)}, u32[]{:S(2)}) collective-permute-start(bf16[4,64,1280]{2,1,0:T(8,128)(2,1)} %get-tuple-element.101), channel_id=1, source_target_pairs={{0,1},{1,0},{2,3},{3,2},{4,5},{5,4},{6,7},{7,6},{8,9},{9,8},{10,11... | collective-permute-start | bytes 1966088 | tf_op jit(solution)/shard_map/ppermute | solution.py:366
  68.0 43.3 %collective-permute-start.10 = (bf16[4,64,1280]{2,1,0:T(8,128)(2,1)}, bf16[4,64,1280]{2,1,0:T(8,128)(2,1)S(1)}, u32[]{:S(2)}, u32[]{:S(2)}) collective-permute-start(bf16[4,64,1280]{2,1,0:T(8,128)(2,1)} %get-tuple-element.103), channel_id=1, source_target_pairs={{0,1},{1,0},{2,3},{3,2},{4,5},{5,4},{6,7},{7,6},{8,9},{9,8},{10,11... | collective-permute-start | bytes 1966088 | tf_op jit(solution)/shard_map/ppermute | solution.py:366
  83.2 64.8 %collective-permute-start.15 = (bf16[4,2,40,1280]{3,2,0,1:T(8,128)(2,1)S(1)}, bf16[4,2,40,1280]{3,2,0,1:T(8,128)(2,1)}, u32[]{:S(2)}, u32[]{:S(2)}) collective-permute-start(bf16[4,2,40,1280]{3,2,0,1:T(8,128)(2,1)S(1)} %maximum_select_fusion.2), channel_id=1, source_target_pairs={{0,16},{8,24},{16,0},{24,8},{1,17},{9,25},{17,1},{25,9},{2,18},{10... | collective-permute-start | bytes 2457608 | tf_op jit(solution)/shard_map/ppermute | solution.py:366
  86.6 100.6 %collective-permute-start.29 = (bf16[4,2,40,1280]{3,2,1,0:T(8,128)(2,1)}, bf16[4,2,40,1280]{3,2,1,0:T(8,128)(2,1)}, u32[]{:S(2)}, u32[]{:S(2)}) collective-permute-start(bf16[4,2,40,1280]{3,2,1,0:T(8,128)(2,1)} %copy_select_fusion), channel_id=1, source_target_pairs={{0,16},{8,24},{16,0},{24,8},{1,17},{9,25},{17,1},{25,9},{2,18},{10... | collective-permute-start | bytes 2457608 | tf_op jit(solution)/shard_map/ppermute | solution.py:366
  88.2 102.2 %collective-permute-start.22 = (bf16[4,2,40,1280]{3,2,1,0:T(8,128)(2,1)}, bf16[4,2,40,1280]{3,2,1,0:T(8,128)(2,1)}, u32[]{:S(2)}, u32[]{:S(2)}) collective-permute-start(bf16[4,2,40,1280]{3,2,1,0:T(8,128)(2,1)} %maximum_select_fusion.3), channel_id=1, source_target_pairs={{0,16},{8,24},{16,0},{24,8},{1,17},{9,25},{17,1},{25,9},{2,18},{10... | collective-permute-start | bytes 2457608 | tf_op jit(solution)/shard_map/ppermute | solution.py:366
  111.3 28.4 %collective-permute-start.4 = (bf16[8,48,480]{2,1,0:T(8,128)(2,1)}, bf16[8,48,480]{2,1,0:T(8,128)(2,1)S(1)}, u32[]{:S(2)}, u32[]{:S(2)}) collective-permute-start(bf16[8,48,480]{2,1,0:T(8,128)(2,1)} %all-to-all-done), channel_id=1, source_target_pairs={{0,16},{8,24},{16,0},{24,8},{1,17},{9,25},{17,1},{25,9},{2,18},{10... | collective-permute-start | bytes 1105928 | tf_op jit(solution)/shard_map/ppermute | solution.py:366
  113.0 35.0 %collective-permute-start.6 = (bf16[8,48,480]{2,1,0:T(8,128)(2,1)}, bf16[8,48,480]{2,1,0:T(8,128)(2,1)S(1)}, u32[]{:S(2)}, u32[]{:S(2)}) collective-permute-start(bf16[8,48,480]{2,1,0:T(8,128)(2,1)} %all-to-all-done), channel_id=1, source_target_pairs={{0,8},{8,0},{16,24},{24,16},{1,9},{9,1},{17,25},{25,17},{2,10},{10... | collective-permute-start | bytes 1105928 | tf_op jit(solution)/shard_map/ppermute | solution.py:366
  139.7 9.2 %collective-permute-start.5 = (bf16[8,48,480]{2,1,0:T(8,128)(2,1)S(1)}, bf16[8,48,480]{2,1,0:T(8,128)(2,1)S(1)}, u32[]{:S(2)}, u32[]{:S(2)}) collective-permute-start(bf16[8,48,480]{2,1,0:T(8,128)(2,1)S(1)} %collective-permute-done.4), channel_id=1, source_target_pairs={{0,8},{8,0},{16,24},{24,16},{1,9},{9,1},{17,25},{25,17},{2,10},{10... | collective-permute-start | bytes 1105928 | tf_op jit(solution)/shard_map/ppermute | solution.py:366
  148.0 42.4 %collective-permute-start.17 = (bf16[4,2,40,1280]{3,2,1,0:T(8,128)(2,1)}, bf16[4,2,40,1280]{3,2,1,0:T(8,128)(2,1)}, u32[]{:S(2)}, u32[]{:S(2)}) collective-permute-start(bf16[4,2,40,1280]{3,2,1,0:T(8,128)(2,1)} %copy.247), channel_id=1, source_target_pairs={{0,8},{8,0},{16,24},{24,16},{1,9},{9,1},{17,25},{25,17},{2,10},{10... | collective-permute-start | bytes 2457608 | tf_op jit(solution)/shard_map/ppermute | solution.py:366
  148.1 42.8 %collective-permute-start.16 = (bf16[4,2,40,1280]{3,2,0,1:T(8,128)(2,1)}, bf16[4,2,40,1280]{3,2,0,1:T(8,128)(2,1)}, u32[]{:S(2)}, u32[]{:S(2)}) collective-permute-start(bf16[4,2,40,1280]{3,2,0,1:T(8,128)(2,1)} %collective-permute-done.15), channel_id=1, source_target_pairs={{0,8},{8,0},{16,24},{24,16},{1,9},{9,1},{17,25},{25,17},{2,10},{10... | collective-permute-start | bytes 2457608 | tf_op jit(solution)/shard_map/ppermute | solution.py:366
  164.8 18.5 %all-to-all-start.1 = ((bf16[8,2,64,160]{3,2,1,0:T(8,128)(2,1)}), bf16[8,2,64,160]{3,2,1,0:T(8,128)(2,1)}, u32[]{:S(2)}, u32[]{:S(2)}) async-start(bf16[8,2,64,160]{3,2,1,0:T(8,128)(2,1)} %copy.243), calls=%async_computation.1 | async-start | bytes 1048576 | tf_op jit(solution)/shard_map/all_to_all | solution.py:472
  173.1 26.1 %collective-permute-start.31 = (bf16[4,2,40,1280]{3,2,1,0:T(8,128)(2,1)}, bf16[4,2,40,1280]{3,2,1,0:T(8,128)(2,1)}, u32[]{:S(2)}, u32[]{:S(2)}) collective-permute-start(bf16[4,2,40,1280]{3,2,1,0:T(8,128)(2,1)} %copy_select_fusion), channel_id=1, source_target_pairs={{0,8},{8,0},{16,24},{24,16},{1,9},{9,1},{17,25},{25,17},{2,10},{10... | collective-permute-start | bytes 2457608 | tf_op jit(solution)/shard_map/ppermute | solution.py:366
  187.2 8.4 %collective-permute-start.24 = (bf16[4,2,40,1280]{3,2,1,0:T(8,128)(2,1)}, bf16[4,2,40,1280]{3,2,1,0:T(8,128)(2,1)S(1)}, u32[]{:S(2)}, u32[]{:S(2)}) collective-permute-start(bf16[4,2,40,1280]{3,2,1,0:T(8,128)(2,1)} %maximum_select_fusion.3), channel_id=1, source_target_pairs={{0,8},{8,0},{16,24},{24,16},{1,9},{9,1},{17,25},{25,17},{2,10},{10... | collective-permute-start | bytes 2457608 | tf_op jit(solution)/shard_map/ppermute | solution.py:366
  190.4 8.8 %collective-permute-start.30 = (bf16[4,2,40,1280]{3,2,1,0:T(8,128)(2,1)}, bf16[4,2,40,1280]{3,2,1,0:T(8,128)(2,1)S(1)}, u32[]{:S(2)}, u32[]{:S(2)}) collective-permute-start(bf16[4,2,40,1280]{3,2,1,0:T(8,128)(2,1)} %collective-permute-done.29), channel_id=1, source_target_pairs={{0,8},{8,0},{16,24},{24,16},{1,9},{9,1},{17,25},{25,17},{2,10},{10... | collective-permute-start | bytes 2457608 | tf_op jit(solution)/shard_map/ppermute | solution.py:366
  190.5 5.2 %collective-permute-start.23 = (bf16[4,2,40,1280]{3,2,1,0:T(8,128)(2,1)}, bf16[4,2,40,1280]{3,2,1,0:T(8,128)(2,1)S(1)}, u32[]{:S(2)}, u32[]{:S(2)}) collective-permute-start(bf16[4,2,40,1280]{3,2,1,0:T(8,128)(2,1)} %collective-permute-done.22), channel_id=1, source_target_pairs={{0,8},{8,0},{16,24},{24,16},{1,9},{9,1},{17,25},{25,17},{2,10},{10... | collective-permute-start | bytes 2457608 | tf_op jit(solution)/shard_map/ppermute | solution.py:366
  213.9 31.9 %all-to-all-start.2 = ((bf16[8,128,160]{1,2,0:T(8,128)(2,1)}), bf16[8,128,160]{1,2,0:T(8,128)(2,1)}, u32[]{:S(2)}, u32[]{:S(2)}) async-start(bf16[8,128,160]{1,2,0:T(8,128)(2,1)} %bitcast.423), calls=%async_computation.2 | async-start | bytes 655360 | tf_op jit(solution)/shard_map/all_to_all | solution.py:499
  226.9 12.8 %collective-permute-start.47 = (bf16[3,128,640]{2,1,0:T(8,128)(2,1)}, bf16[3,128,640]{2,1,0:T(8,128)(2,1)}, u32[]{:S(2)}, u32[]{:S(2)}) collective-permute-start(bf16[3,128,640]{2,1,0:T(8,128)(2,1)} %bitcast.383), channel_id=1, source_target_pairs={{0,16},{8,24},{16,0},{24,8},{1,17},{9,25},{17,1},{25,9},{2,18},{10... | collective-permute-start | bytes 1474568 | tf_op jit(solution)/shard_map/ppermute | solution.py:366
  233.3 62.1 %collective-permute-start.45 = (bf16[128,3840]{1,0:T(8,128)(2,1)}, bf16[128,3840]{1,0:T(8,128)(2,1)}, u32[]{:S(2)}, u32[]{:S(2)}) collective-permute-start(bf16[128,3840]{1,0:T(8,128)(2,1)} %pad_maximum_fusion.9), channel_id=1, source_target_pairs={{0,16},{8,24},{16,0},{24,8},{1,17},{9,25},{17,1},{25,9},{2,18},{10... | collective-permute-start | bytes 2949128 | tf_op jit(solution)/shard_map/ppermute | solution.py:366
  243.9 107.0 %collective-permute-start.48 = (bf16[3,256,320]{1,2,0:T(8,128)(2,1)}, bf16[3,256,320]{1,2,0:T(8,128)(2,1)}, u32[]{:S(2)}, u32[]{:S(2)}) collective-permute-start(bf16[3,256,320]{1,2,0:T(8,128)(2,1)} %get-tuple-element.82), channel_id=1, source_target_pairs={{0,8},{8,0},{16,24},{24,16},{1,9},{9,1},{17,25},{25,17},{2,10},{10... | collective-permute-start | bytes 1474568 | tf_op jit(solution)/shard_map/ppermute | solution.py:366
  278.6 4.9 %collective-permute-start.57 = (f32[5,1280]{1,0:T(8,128)S(1)}, f32[5,1280]{1,0:T(8,128)S(1)}, u32[]{:S(2)}, u32[]{:S(2)}) collective-permute-start(f32[5,1280]{1,0:T(8,128)S(1)} %add.290), channel_id=1, source_target_pairs={{0,16},{8,24},{16,0},{24,8},{1,17},{9,25},{17,1},{25,9},{2,18},{10... | collective-permute-start | bytes 76808 | tf_op jit(solution)/shard_map/ppermute | solution.py:366
  283.5 2.9 collective-permute-start.58
  284.8 16.5 %collective-permute-start.40 = (bf16[8,2,40,480]{3,2,1,0:T(8,128)(2,1)S(1)}, bf16[8,2,40,480]{3,2,1,0:T(8,128)(2,1)S(1)}, u32[]{:S(2)}, u32[]{:S(2)}) collective-permute-start(bf16[8,2,40,480]{3,2,1,0:T(8,128)(2,1)S(1)} %dynamic-slice_bitcast_fusion.1), channel_id=1, source_target_pairs={{0,8},{8,0},{16,24},{24,16},{1,9},{9,1},{17,25},{25,17},{2,10},{10... | collective-permute-start | bytes 1843208 | tf_op jit(solution)/shard_map/ppermute | solution.py:366
  286.4 2.9 collective-permute-start.59
  286.5 16.6 %collective-permute-start.32 = (bf16[4,64,1280]{2,1,0:T(8,128)(2,1)S(1)}, bf16[4,64,1280]{2,1,0:T(8,128)(2,1)S(1)}, u32[]{:S(2)}, u32[]{:S(2)}) collective-permute-start(bf16[4,64,1280]{2,1,0:T(8,128)(2,1)S(1)} %dynamic-slice_bitcast_fusion.3), channel_id=1, source_target_pairs={{0,1},{1,0},{2,3},{3,2},{4,5},{5,4},{6,7},{7,6},{8,9},{9,8},{10,11... | collective-permute-start | bytes 1966088 | tf_op jit(solution)/shard_map/ppermute | solution.py:366
  289.3 3.8 collective-permute-start.60
  293.0 21.9 %collective-permute-start.36 = (bf16[4,64,1280]{2,1,0:T(8,128)(2,1)S(1)}, bf16[4,64,1280]{2,1,0:T(8,128)(2,1)S(1)}, u32[]{:S(2)}, u32[]{:S(2)}) collective-permute-start(bf16[4,64,1280]{2,1,0:T(8,128)(2,1)S(1)} %dynamic-slice_bitcast_fusion.2), channel_id=1, source_target_pairs={{0,1},{1,0},{2,3},{3,2},{4,5},{5,4},{6,7},{7,6},{8,9},{9,8},{10,11... | collective-permute-start | bytes 1966088 | tf_op jit(solution)/shard_map/ppermute | solution.py:366
  296.7 41.7 %collective-permute-start.46 = (bf16[256,3840]{1,0:T(8,128)(2,1)S(1)}, bf16[256,3840]{1,0:T(8,128)(2,1)S(1)}, u32[]{:S(2)}, u32[]{:S(2)}) collective-permute-start(bf16[256,3840]{1,0:T(8,128)(2,1)S(1)} %pad_maximum_fusion.5), channel_id=1, source_target_pairs={{0,8},{8,0},{16,24},{24,16},{1,9},{9,1},{17,25},{25,17},{2,10},{10... | collective-permute-start | bytes 5898248 | tf_op jit(solution)/shard_map/ppermute | solution.py:366
  303.3 14.0 %collective-permute-start.33 = (bf16[64,1280]{1,0:T(8,128)(2,1)S(1)}, bf16[64,1280]{1,0:T(8,128)(2,1)S(1)}, u32[]{:S(2)}, u32[]{:S(2)}) collective-permute-start(bf16[64,1280]{1,0:T(8,128)(2,1)S(1)} %get-tuple-element.95), channel_id=1, source_target_pairs={{0,2},{1,3},{2,0},{3,1},{4,6},{5,7},{6,4},{7,5},{8,10},{9,11},{10,... | collective-permute-start | bytes 491528 | tf_op jit(solution)/shard_map/ppermute | solution.py:366
  303.6 14.9 %collective-permute-start.34 = (bf16[64,1280]{1,0:T(8,128)(2,1)S(1)}, bf16[64,1280]{1,0:T(8,128)(2,1)S(1)}, u32[]{:S(2)}, u32[]{:S(2)}) collective-permute-start(bf16[64,1280]{1,0:T(8,128)(2,1)S(1)} %get-tuple-element.97), channel_id=1, source_target_pairs={{0,4},{1,5},{2,6},{3,7},{4,0},{5,1},{6,2},{7,3},{8,12},{9,13},{10,... | collective-permute-start | bytes 491528 | tf_op jit(solution)/shard_map/ppermute | solution.py:366
  314.9 7.0 %collective-permute-start.35 = (bf16[64,1280]{1,0:T(8,128)(2,1)S(1)}, bf16[64,1280]{1,0:T(8,128)(2,1)S(1)}, u32[]{:S(2)}, u32[]{:S(2)}) collective-permute-start(bf16[64,1280]{1,0:T(8,128)(2,1)S(1)} %get-tuple-element.96), channel_id=1, source_target_pairs={{0,6},{1,7},{2,4},{3,5},{4,2},{5,3},{6,0},{7,1},{8,14},{9,15},{10,... | collective-permute-start | bytes 491528 | tf_op jit(solution)/shard_map/ppermute | solution.py:366
  317.3 6.4 %collective-permute-start.37 = (bf16[64,1280]{1,0:T(8,128)(2,1)S(1)}, bf16[64,1280]{1,0:T(8,128)(2,1)S(1)}, u32[]{:S(2)}, u32[]{:S(2)}) collective-permute-start(bf16[64,1280]{1,0:T(8,128)(2,1)S(1)} %get-tuple-element.98), channel_id=1, source_target_pairs={{0,2},{1,3},{2,0},{3,1},{4,6},{5,7},{6,4},{7,5},{8,10},{9,11},{10,... | collective-permute-start | bytes 491528 | tf_op jit(solution)/shard_map/ppermute | solution.py:366
  318.5 14.5 %collective-permute-start.38 = (bf16[64,1280]{1,0:T(8,128)(2,1)S(1)}, bf16[64,1280]{1,0:T(8,128)(2,1)S(1)}, u32[]{:S(2)}, u32[]{:S(2)}) collective-permute-start(bf16[64,1280]{1,0:T(8,128)(2,1)S(1)} %get-tuple-element.100), channel_id=1, source_target_pairs={{0,4},{1,5},{2,6},{3,7},{4,0},{5,1},{6,2},{7,3},{8,12},{9,13},{10,... | collective-permute-start | bytes 491528 | tf_op jit(solution)/shard_map/ppermute | solution.py:366
  321.9 15.7 %collective-permute-start.39 = (bf16[64,1280]{1,0:T(8,128)(2,1)S(1)}, bf16[64,1280]{1,0:T(8,128)(2,1)S(1)}, u32[]{:S(2)}, u32[]{:S(2)}) collective-permute-start(bf16[64,1280]{1,0:T(8,128)(2,1)S(1)} %get-tuple-element.99), channel_id=1, source_target_pairs={{0,6},{1,7},{2,4},{3,5},{4,2},{5,3},{6,0},{7,1},{8,14},{9,15},{10,... | collective-permute-start | bytes 491528 | tf_op jit(solution)/shard_map/ppermute | solution.py:366
  323.7 35.7 %collective-permute-start.41 = (bf16[8,40,480]{2,1,0:T(8,128)(2,1)}, bf16[8,40,480]{2,1,0:T(8,128)(2,1)}, u32[]{:S(2)}, u32[]{:S(2)}) collective-permute-start(bf16[8,40,480]{2,1,0:T(8,128)(2,1)} %dynamic-slice_bitcast_fusion.7), channel_id=1, source_target_pairs={{0,16},{8,24},{16,0},{24,8},{1,17},{9,25},{17,1},{25,9},{2,18},{10... | collective-permute-start | bytes 921608 | tf_op jit(solution)/shard_map/ppermute | solution.py:366
  358.3 45.9 %collective-permute-start.49 = (bf16[4,3,160,320]{3,2,0,1:T(8,128)(2,1)}, bf16[4,3,160,320]{3,2,0,1:T(8,128)(2,1)}, u32[]{:S(2)}, u32[]{:S(2)}) collective-permute-start(bf16[4,3,160,320]{3,2,0,1:T(8,128)(2,1)} %dynamic-slice_bitcast_fusion), channel_id=1, source_target_pairs={{0,1},{1,0},{2,3},{3,2},{4,5},{5,4},{6,7},{7,6},{8,9},{9,8},{10,11... | collective-permute-start | bytes 3686408 | tf_op jit(solution)/shard_map/ppermute | solution.py:366
  361.2 32.5 %all-to-all-start.3 = ((bf16[8,40,480]{2,1,0:T(8,128)(2,1)}), bf16[8,40,480]{2,1,0:T(8,128)(2,1)}, u32[]{:S(2)}, u32[]{:S(2)}) async-start(bf16[8,40,480]{2,1,0:T(8,128)(2,1)} %fusion.30), calls=%async_computation.3 | async-start | bytes 655360 | tf_op jit(solution)/shard_map/all_to_all | solution.py:550
  393.8 6.2 %collective-permute-start.42 = (bf16[8,40,480]{2,1,0:T(8,128)(2,1)}, bf16[8,40,480]{2,1,0:T(8,128)(2,1)}, u32[]{:S(2)}, u32[]{:S(2)}) collective-permute-start(bf16[8,40,480]{2,1,0:T(8,128)(2,1)} %all-to-all-done.3), channel_id=1, source_target_pairs={{0,16},{8,24},{16,0},{24,8},{1,17},{9,25},{17,1},{25,9},{2,18},{10... | collective-permute-start | bytes 921608 | tf_op jit(solution)/shard_map/ppermute | solution.py:366
  394.2 18.2 %collective-permute-start.44 = (bf16[8,40,480]{2,1,0:T(8,128)(2,1)}, bf16[8,40,480]{2,1,0:T(8,128)(2,1)S(1)}, u32[]{:S(2)}, u32[]{:S(2)}) collective-permute-start(bf16[8,40,480]{2,1,0:T(8,128)(2,1)} %all-to-all-done.3), channel_id=1, source_target_pairs={{0,8},{8,0},{16,24},{24,16},{1,9},{9,1},{17,25},{25,17},{2,10},{10... | collective-permute-start | bytes 921608 | tf_op jit(solution)/shard_map/ppermute | solution.py:366
  400.0 12.3 %collective-permute-start.43 = (bf16[8,40,480]{2,1,0:T(8,128)(2,1)}, bf16[8,40,480]{2,1,0:T(8,128)(2,1)S(1)}, u32[]{:S(2)}, u32[]{:S(2)}) collective-permute-start(bf16[8,40,480]{2,1,0:T(8,128)(2,1)} %collective-permute-done.42), channel_id=1, source_target_pairs={{0,8},{8,0},{16,24},{24,16},{1,9},{9,1},{17,25},{25,17},{2,10},{10... | collective-permute-start | bytes 921608 | tf_op jit(solution)/shard_map/ppermute | solution.py:366
  408.6 15.9 %collective-permute-start.50 = (bf16[3,160,320]{2,1,0:T(8,128)(2,1)}, bf16[3,160,320]{2,1,0:T(8,128)(2,1)S(1)}, u32[]{:S(2)}, u32[]{:S(2)}) collective-permute-start(bf16[3,160,320]{2,1,0:T(8,128)(2,1)} %get-tuple-element.69), channel_id=1, source_target_pairs={{0,2},{1,3},{2,0},{3,1},{4,6},{5,7},{6,4},{7,5},{8,10},{9,11},{10,... | collective-permute-start | bytes 921608 | tf_op jit(solution)/shard_map/ppermute | solution.py:366
  408.6 19.2 %collective-permute-start.51 = (bf16[3,160,320]{2,1,0:T(8,128)(2,1)}, bf16[3,160,320]{2,1,0:T(8,128)(2,1)}, u32[]{:S(2)}, u32[]{:S(2)}) collective-permute-start(bf16[3,160,320]{2,1,0:T(8,128)(2,1)} %get-tuple-element.71), channel_id=1, source_target_pairs={{0,4},{1,5},{2,6},{3,7},{4,0},{5,1},{6,2},{7,3},{8,12},{9,13},{10,... | collective-permute-start | bytes 921608 | tf_op jit(solution)/shard_map/ppermute | solution.py:366
  410.8 33.0 %collective-permute-start.52 = (bf16[3,160,320]{2,1,0:T(8,128)(2,1)S(1)}, bf16[3,160,320]{2,1,0:T(8,128)(2,1)}, u32[]{:S(2)}, u32[]{:S(2)}) collective-permute-start(bf16[3,160,320]{2,1,0:T(8,128)(2,1)S(1)} %get-tuple-element.70), channel_id=1, source_target_pairs={{0,6},{1,7},{2,4},{3,5},{4,2},{5,3},{6,0},{7,1},{8,14},{9,15},{10,... | collective-permute-start | bytes 921608 | tf_op jit(solution)/shard_map/ppermute | solution.py:366
  446.0 9.3 %collective-permute-start.53 = (bf16[3,160,320]{2,1,0:T(8,128)(2,1)}, bf16[3,160,320]{2,1,0:T(8,128)(2,1)}, u32[]{:S(2)}, u32[]{:S(2)}) collective-permute-start(bf16[3,160,320]{2,1,0:T(8,128)(2,1)} %fusion.29), channel_id=1, source_target_pairs={{0,16},{8,24},{16,0},{24,8},{1,17},{9,25},{17,1},{25,9},{2,18},{10... | collective-permute-start | bytes 921608 | tf_op jit(solution)/shard_map/ppermute | solution.py:366
  448.6 21.1 %collective-permute-start.55 = (bf16[3,160,320]{2,1,0:T(8,128)(2,1)}, bf16[3,160,320]{2,1,0:T(8,128)(2,1)}, u32[]{:S(2)}, u32[]{:S(2)}) collective-permute-start(bf16[3,160,320]{2,1,0:T(8,128)(2,1)} %fusion.29), channel_id=1, source_target_pairs={{0,8},{8,0},{16,24},{24,16},{1,9},{9,1},{17,25},{25,17},{2,10},{10... | collective-permute-start | bytes 921608 | tf_op jit(solution)/shard_map/ppermute | solution.py:366
  455.3 14.4 %collective-permute-start.54 = (bf16[3,160,320]{2,1,0:T(8,128)(2,1)}, bf16[3,160,320]{2,1,0:T(8,128)(2,1)}, u32[]{:S(2)}, u32[]{:S(2)}) collective-permute-start(bf16[3,160,320]{2,1,0:T(8,128)(2,1)} %collective-permute-done.53), channel_id=1, source_target_pairs={{0,8},{8,0},{16,24},{24,16},{1,9},{9,1},{17,25},{25,17},{2,10},{10... | collective-permute-start | bytes 921608 | tf_op jit(solution)/shard_map/ppermute | solution.py:366
  (86 other events, 613.9 us)

commit v2 on v0

--- a/solution.py
+++ b/solution.py
@@ -1,8 +1,11 @@
+import functools
 import math
 
 import jax
 import jax.numpy as jnp
 from jax import lax
+from jax.experimental import pallas as pl
+from jax.experimental.pallas import tpu as pltpu
 from jax.sharding import PartitionSpec as P
 
 EPS = 1e-06
@@ -362,9 +365,493 @@
     )
 
 
+LOW, WIDE = jnp.bfloat16, jnp.float32
+VMEM_BYTES = 48 * 1024 * 1024
+
+
+def swap(value, axis, bit, size):
+    return lax.ppermute(value, axis, [(i, i ^ bit) for i in range(size)])
+
+
+def in_order(pieces, index):
+    low, high = (index & 1) == 1, (index & 2) == 2
+    half = [jnp.where(low, pieces[p ^ 1], pieces[p]) for p in range(4)]
+    return [jnp.where(high, half[p ^ 2], half[p]) for p in range(4)]
+
+
+def over_grp(value):
+    far = swap(value, "grp", 2, 4)
+    return [value, swap(value, "grp", 1, 4), far, swap(far, "grp", 1, 4)]
+
+
+def over_z(value, z):
+    return jnp.stack(in_order([value] + [swap(value, "seq", 2 * k, 8) for k in (1, 2, 3)], z))
+
+
+def gather_seq(value, z, y):
+    mine = over_z(value, z)
+    other = swap(mine, "seq", 1, 8)
+    return jnp.where(y == 0, jnp.stack([mine, other], 1), jnp.stack([other, mine], 1))
+
+
+def nn(a, b):
+    return lax.dot_general(a, b, (((1,), (0,)), ((), ())), preferred_element_type=WIDE)
+
+
+def nt(a, b):
+    return lax.dot_general(a, b, (((1,), (1,)), ((), ())), preferred_element_type=WIDE)
+
+
+def tn(a, b):
+    return lax.dot_general(a, b, (((0,), (0,)), ((), ())), preferred_element_type=WIDE)
+
+
+SMEM = pl.BlockSpec(memory_space=pltpu.SMEM)
+VMEM = pl.BlockSpec(memory_space=pltpu.VMEM)
+ANY = pl.BlockSpec(memory_space=pl.ANY)
+
+
+def call(body, outs, ins, scratch=(), flops=0, **more):
+    moved = sum(a.size * a.dtype.itemsize for a, _ in ins)
+    return pl.pallas_call(
+        body,
+        out_shape=outs,
+        in_specs=[spec for _, spec in ins],
+        out_specs=jax.tree.map(lambda _: VMEM, outs),
+        scratch_shapes=list(scratch),
+        compiler_params=pltpu.CompilerParams(vmem_limit_bytes=VMEM_BYTES),
+        cost_estimate=pl.CostEstimate(flops=flops, bytes_accessed=moved, transcendentals=0),
+        **more,
+    )(*[a for a, _ in ins])
+
+
+def shape(*dims, dtype=LOW):
+    return jax.ShapeDtypeStruct(dims, dtype)
+
+
+def load_tokens(info, mine, other, x, seq, rows):
+    y = info[0]
+    for k in range(4):
+        x[pl.ds((2 * k + y) * rows, rows), :] = mine[k, seq]
+        x[pl.ds((2 * k + 1 - y) * rows, rows), :] = other[k, seq]
+
+
+def project(x, gain, w):
+    wide = x[...].astype(WIDE)
+    inv = lax.rsqrt(jnp.mean(wide * wide, axis=-1, keepdims=True) + EPS)
+    unit = wide * inv
+    normed = (unit * gain[...]).astype(LOW)
+    return unit, normed, nn(normed, w[...])
+
+
+def probabilities(q, k, first, length):
+    scores = nt(q, k)
+    query = first + lax.broadcasted_iota(jnp.int32, scores.shape, 0)
+    key = lax.broadcasted_iota(jnp.int32, scores.shape, 1)
+    scores = jnp.where((key <= query) & (key < length), scores, NEG)
+    raised = jnp.exp(scores - jnp.max(scores, axis=-1, keepdims=True))
+    return raised / jnp.sum(raised, axis=-1, keepdims=True)
+
+
+def attend_kernel(size, info, mine, other, w, gain, scale, out, x):
+    seq_count, rows = mine.shape[1:3]
+    share = out.shape[-1]
+    total = 8 * rows
+    block = total // 2
+    for seq in range(seq_count):
+        load_tokens(info, mine, other, x, seq, rows)
+        _, _, qkv = project(x, gain, w)
+        heads = []
+        for h in range(share // size):
+            at = h * size
+            q = (qkv[:, at : at + size] * scale[...]).astype(LOW)
+            k = qkv[:, share + at : share + at + size].astype(LOW)
+            v = qkv[:, 2 * share + at : 2 * share + at + size].astype(LOW)
+            parts = []
+            for b in range(2):
+                end = (b + 1) * block
+                probs = probabilities(q[b * block : end], k[:end], b * block, info[1 + seq])
+                parts.append(nn(probs.astype(LOW), v[:end]))
+            heads.append(jnp.concatenate(parts, 0))
+        att = jnp.concatenate(heads, 1).astype(LOW)
+        for t in range(8):
+            out[t, seq] = att[t * rows : (t + 1) * rows]
+
+
+def attend_back_kernel(size, seq, info, mine, other, w, gain, scale, ga, *refs):
+    if seq:
+        before, sums_before, keep, send, left, right, sums, x, p_ref, g_ref = refs
+    else:
+        keep, send, grads, sums, x, p_ref = refs
+    rows = mine.shape[2]
+    share = ga.shape[-1]
+    total = 8 * rows
+    block = total // 2
+    width = x.shape[1]
+    y = info[0]
+    load_tokens(info, mine, other, x, seq, rows)
+    unit, normed, qkv = project(x, gain, w)
+    whole = jnp.concatenate([ga[t, seq] for t in range(8)], 0)
+    grad_q, grad_k, grad_v, grad_scale = [], [], [], jnp.zeros((1, size), WIDE)
+    for h in range(share // size):
+        at = h * size
+        raw = qkv[:, at : at + size]
+        q = (raw * scale[...]).astype(LOW)
+        k = qkv[:, share + at : share + at + size].astype(LOW)
+        v = qkv[:, 2 * share + at : 2 * share + at + size].astype(LOW)
+        own = whole[:, at : at + size]
+        gq_parts, gk, gv = [], 0.0, 0.0
+        for b in range(2):
+            start, end = b * block, (b + 1) * block
+            probs = probabilities(q[start:end], k[:end], start, info[1 + seq])
+            grad_probs = nt(own[start:end], v[:end])
+            delta = jnp.sum(grad_probs * probs, axis=-1, keepdims=True)
+            grad_scores = (probs * (grad_probs - delta)).astype(LOW)
+            gq_parts.append(nn(grad_scores, k[:end]))
+            gk_new = tn(grad_scores, q[start:end])
+            gv_new = tn(probs.astype(LOW), own[start:end])
+            if b:
+                gk = gk_new + jnp.concatenate([gk, jnp.zeros_like(gk)], 0)
+                gv = gv_new + jnp.concatenate([gv, jnp.zeros_like(gv)], 0)
+            else:
+                gk, gv = gk_new, gv_new
+        gq = jnp.concatenate(gq_parts, 0).astype(LOW).astype(WIDE)
+        grad_scale = grad_scale + jnp.sum(gq * raw, axis=0, keepdims=True)
+        grad_q.append(gq * scale[...])
+        grad_k.append(gk)
+        grad_v.append(gv)
+    pad = jnp.zeros((total, w.shape[1] - 3 * share), WIDE)
+    grads_all = jnp.concatenate(grad_q + grad_k + grad_v + [pad], 1).astype(LOW)
+    partial = nt(grads_all, w[...])
+    gain_grad = jnp.sum(partial * unit, axis=0, keepdims=True)
+    scale_row = jnp.concatenate([grad_scale, jnp.zeros((1, width - size), WIDE)], 1)
+    p_ref[...] = partial.astype(WIDE)
+    for k in range(4):
+        keep[k] = p_ref[pl.ds((2 * k + y) * rows, rows), :].astype(LOW)
+        send[k] = p_ref[pl.ds((2 * k + 1 - y) * rows, rows), :].astype(LOW)
+    result = tn(normed, grads_all)
+    if not seq:
+        grads[...] = result
+        sums[...] = jnp.concatenate([gain_grad, scale_row, jnp.zeros((6, width), WIDE)], 0)
+        return
+    sums[...] = sums_before[...] + jnp.concatenate([gain_grad, scale_row, jnp.zeros((6, width), WIDE)], 0)
+    g_ref[...] = result + before[...]
+    c = info[4]
+    piece = share // 4
+    for t in range(8):
+        for half in range(2):
+            base = t * share + 2 * half * piece
+            left[t, half] = g_ref[pl.ds(base + c * piece, piece), :].astype(LOW)
+            right[t, half] = g_ref[pl.ds(base + (1 - c) * piece, piece), :].astype(LOW)
+
+
+def feed_kernel(rows, info, att, tokens, cotangent, gains, *refs):
+    blocks, refs = refs[:12], refs[12:]
+    layer_out, grad_hidden_out, ga, left, keep, send, sums, w_out, w_up, w_down, sems = refs
+    x, g = info[3], info[5]
+    piece = blocks[0].shape[0]
+    copies = []
+    for j, w in enumerate((w_out, w_up, w_down)):
+        for k in range(4):
+            target = w.at[pl.ds(pl.multiple_of((g ^ k) * piece, piece), piece), :]
+            copies.append(pltpu.make_async_copy(blocks[4 * j + k], target, sems.at[j, k]))
+            copies[-1].start()
+
+    def arrived(j):
+        for k in range(4):
+            copies[4 * j + k].wait()
+
+    gain, bias_up, bias_down = gains[1:2], gains[2:3], gains[3:4]
+    attended = jnp.concatenate([att[t] for t in range(8)], 1)
+    wide = tokens[...].astype(WIDE)
+    count, width = wide.shape
+    arrived(0)
+    hidden = wide + nn(attended, w_out[...])
+    inv = lax.rsqrt(jnp.mean(hidden * hidden, axis=-1, keepdims=True) + EPS)
+    normed = (hidden * inv * gain).astype(LOW)
+    arrived(1)
+    pre = nn(normed, w_up[...]) + bias_up
+    sigma = jax.nn.sigmoid(pre)
+    act = (pre * sigma).astype(LOW)
+    arrived(2)
+    layer_out[...] = (hidden + nn(act, w_down[...]) + bias_down).astype(LOW)
+    row = lax.broadcasted_iota(jnp.int32, (count, 1), 0)
+    at = info[6] * rows + jnp.where(row < rows, row, row - rows)
+    valid = at < jnp.where(row < rows, info[1], info[2])
+    grad_out = jnp.where(valid, cotangent[...].astype(WIDE), 0.0)
+    grad_out_low = grad_out.astype(LOW)
+    grad_act = nt(grad_out_low, w_down[...])
+    grad_pre = (grad_act * sigma * (1.0 + pre * (1.0 - sigma))).astype(LOW)
+    grad_normed = nt(grad_pre, w_up[...])
+    weighted = grad_normed * gain
+    grad_hidden = (
+        grad_out
+        + inv * weighted
+        - hidden * (inv * inv * inv) * jnp.mean(weighted * hidden, axis=-1, keepdims=True)
+    )
+    grad_mixed = grad_hidden.astype(LOW)
+    grad_hidden_out[...] = grad_hidden
+    grad_att = nt(grad_mixed, w_out[...])
+    share = ga.shape[-1]
+    for t in range(8):
+        ga[t] = grad_att[:, t * share : (t + 1) * share].astype(LOW)
+    half = width // 2
+    for j, (a, b) in enumerate(((attended, grad_mixed), (normed, grad_pre), (act, grad_out_low))):
+        left[:, j * width : (j + 1) * width] = a
+        first, second = b[:, :half], b[:, half:]
+        keep[:, j * half : (j + 1) * half] = jnp.where(x == 0, first, second)
+        send[:, j * half : (j + 1) * half] = jnp.where(x == 0, second, first)
+    zeros = jnp.zeros((5, width), WIDE)
+    sums[...] = jnp.concatenate(
+        [
+            jnp.sum(grad_normed * hidden * inv, axis=0, keepdims=True),
+            jnp.sum(grad_pre.astype(WIDE), axis=0, keepdims=True),
+            jnp.sum(grad_out, axis=0, keepdims=True),
+            zeros,
+        ],
+        0,
+    )
+
+
+def weight_grad_kernel(info, *refs):
+    lefts, rights, (keep, send, result) = refs[:4], refs[4:8], refs[8:]
+    c, y = info[4], info[0]
+    width = lefts[0].shape[1] // 3
+    half = rights[0].shape[1] // 3
+    quarter = half // 2
+    for j in range(3):
+        a = jnp.concatenate([r[:, j * width : (j + 1) * width] for r in lefts], 0)
+        b = jnp.concatenate([r[:, j * half : (j + 1) * half] for r in rights], 0)
+        b = jnp.where(c == 0, b[:, :quarter], b[:, quarter:])
+        result[:, j * quarter : (j + 1) * quarter] = tn(a, b)
+    share = width // 8
+    for k in range(4):
+        keep[k] = result[pl.ds((2 * k + y) * share, share), :].astype(LOW)
+        send[k] = result[pl.ds((2 * k + 1 - y) * share, share), :].astype(LOW)
+
+
+def add_z_kernel(info, keep, received, own, *sends):
+    z = info[7]
+    own[...] = keep[z].astype(WIDE) + received[z].astype(WIDE)
+    for k, send in enumerate(sends):
+        at = z ^ (k + 1)
+        send[...] = (keep[at].astype(WIDE) + received[at].astype(WIDE)).astype(LOW)
+
+
+def scatter_seq(info, keep, send):
+    received = swap(send, "seq", 1, 8)
+    part = keep.shape[1:]
+    own, *sends = call(
+        add_z_kernel,
+        (shape(*part, dtype=WIDE), shape(*part), shape(*part), shape(*part)),
+        [(info, SMEM), (keep, VMEM), (received, VMEM)],
+    )
+    return [own] + [swap(v, "seq", 2 * (k + 1), 8) for k, v in enumerate(sends)]
+
+
+def add_all(parts):
+    return sum(p.astype(WIDE) for p in parts[1:]) + parts[0]
+
+
+def tokens_kernel(tokens, gain, grad_hidden, *refs):
+    out, parts = refs[-1], refs[:-1]
+    rows = out.shape[1]
+    for seq in range(out.shape[0]):
+        grad = parts[4 * seq][...]
+        for part in parts[4 * seq + 1 : 4 * seq + 4]:
+            grad = grad + part[...].astype(WIDE)
+        wide = tokens[seq].astype(WIDE)
+        inv = lax.rsqrt(jnp.mean(wide * wide, axis=-1, keepdims=True) + EPS)
+        weighted = grad * gain[...]
+        out[seq] = (
+            grad_hidden[seq]
+            + inv * weighted
+            - wide * (inv * inv * inv) * jnp.mean(weighted * wide, axis=-1, keepdims=True)
+        )
+
+
+def columns_kernel(info, a, b, c, d, *outs):
+    g = info[5]
+    low, high = (g & 1) == 1, (g & 2) == 2
+    pieces = [r[...].astype(WIDE) for r in (a, b, c, d)]
+    half = [jnp.where(low, pieces[p ^ 1], pieces[p]) for p in range(4)]
+    pieces = [jnp.where(high, half[p ^ 2], half[p]) for p in range(4)]
+    quarter = a.shape[1] // 3
+    for j, out in enumerate(outs):
+        out[...] = jnp.concatenate([p[:, j * quarter : (j + 1) * quarter] for p in pieces], 1)
+
+
+def rows_kernel(share, info, a, b, c, d, *outs):
+    g = info[5]
+    for k, piece in enumerate((a, b, c, d)):
+        count = piece.shape[1]
+        at = pl.ds(pl.multiple_of((g ^ k) * count, 8), count)
+        for j, out in enumerate(outs):
+            out[at, :] = jnp.concatenate(
+                [piece[t, :, j * share : (j + 1) * share].astype(WIDE) for t in range(8)], 1
+            )
+
+
+def payload_kernel(a, b, c, smalls, out):
+    share = a.shape[1] // 8
+    for t in range(8):
+        cols = [r[:, t * share : (t + 1) * share].astype(WIDE) for r in (a, b, c)]
+        out[t] = jnp.concatenate(cols + [smalls[...]], 1).astype(LOW)
+
+
+def quick(
+    tokens,
+    lengths,
+    query_weight,
+    key_weight,
+    value_weight,
+    out_weight,
+    up_weight,
+    down_weight,
+    norm_gain,
+    ff_gain,
+    up_bias,
+    down_bias,
+    query_scale,
+    cotangent,
+):
+    seq_count, rows, width = tokens.shape
+    size = query_scale.shape[0]
+    share = width // 8
+    count = seq_count * rows
+    wide_cols = -(-(3 * share + 4) // 128) * 128
+    wrows = query_weight.shape[0]
+    g, s = lax.axis_index("grp"), lax.axis_index("seq")
+    x, c, z, y = g // 2, g % 2, s // 2, s % 2
+    info = jnp.stack([y, lengths[0], lengths[1], x, c, g, s, z]).astype(jnp.int32)
+
+    smalls = jnp.stack([norm_gain, ff_gain, up_bias, down_bias], 1).astype(WIDE)
+    smalls = jnp.pad(smalls, ((0, 0), (0, wide_cols - 3 * share - 4)))
+    payload = call(
+        payload_kernel,
+        shape(8, wrows, wide_cols),
+        [(query_weight, VMEM), (key_weight, VMEM), (value_weight, VMEM), (smalls, VMEM)],
+    )
+    columns = lax.all_to_all(payload, "seq", 0, 0, tiled=True)
+    mine = over_z(tokens, z)
+    other = swap(mine, "seq", 1, 8)
+    w_qkv = jnp.stack(in_order(over_grp(columns), g)).reshape(width, wide_cols)
+    gains = w_qkv[:, 3 * share : 3 * share + 4].T.astype(WIDE)
+    gain_one = gains[0:1]
+    blocks = []
+    for w in (out_weight, up_weight, down_weight):
+        blocks += [v.reshape(8 * wrows, width) for v in over_grp(gather_seq(w, z, y))]
+    factor = QCONST / math.sqrt(size)
+    scale = (factor * jax.nn.softplus(query_scale)).reshape(1, size)
+
+    att = call(
+        functools.partial(attend_kernel, size),
+        shape(8, seq_count, rows, share),
+        [(info, SMEM), (mine, VMEM), (other, VMEM), (w_qkv, VMEM), (gain_one, VMEM), (scale, VMEM)],
+        [pltpu.VMEM((8 * rows, width), LOW)],
+        flops=2 * seq_count * 8 * rows * width * wide_cols,
+    )
+    att = lax.all_to_all(att, "seq", 0, 0, tiled=True).reshape(8, count, share)
+
+    layer_out, grad_hidden, grad_att, left, keep, send, sums_ff = call(
+        functools.partial(feed_kernel, rows),
+        (
+            shape(count, width),
+            shape(count, width, dtype=WIDE),
+            shape(8, count, share),
+            shape(count, 3 * width),
+            shape(count, 3 * width // 2),
+            shape(count, 3 * width // 2),
+            shape(8, width, dtype=WIDE),
+        ),
+        [
+            (info, SMEM),
+            (att, VMEM),
+            (tokens.reshape(count, width), VMEM),
+            (cotangent.reshape(count, width), VMEM),
+            (gains, VMEM),
+        ]
+        + [(b, ANY) for b in blocks],
+        [pltpu.VMEM((width, width), LOW)] * 3 + [pltpu.SemaphoreType.DMA((3, 4))],
+        flops=14 * count * width * width,
+    )
+    grad_att = lax.all_to_all(grad_att, "seq", 0, 0, tiled=True).reshape(8, seq_count, rows, share)
+
+    lefts = over_grp(left)
+    far = swap(send, "grp", 2, 4)
+    rights = [keep, swap(keep, "grp", 1, 4), far, swap(far, "grp", 1, 4)]
+    keep, send = call(
+        weight_grad_kernel,
+        (shape(4, share, 3 * width // 4), shape(4, share, 3 * width // 4)),
+        [(info, SMEM)] + [(v, VMEM) for v in lefts + rights],
+        [pltpu.VMEM((width, 3 * width // 4), WIDE)],
+        flops=6 * 4 * count * width * width // 4,
+    )
+    ff_part = add_all(scatter_seq(info, keep, send)).astype(LOW)
+    whole = shape(share, width, dtype=WIDE)
+    ff_grads = call(
+        columns_kernel, (whole, whole, whole), [(info, SMEM)] + [(v, VMEM) for v in over_grp(ff_part)]
+    )
+
+    parts, carried = [], []
+    for seq in range(seq_count):
+        scratch = [pltpu.VMEM((8 * rows, width), LOW), pltpu.VMEM((8 * rows, width), WIDE)]
+        outs = [shape(4, rows, width), shape(4, rows, width)]
+        if seq:
+            scratch.append(pltpu.VMEM((width, wide_cols), WIDE))
+            outs += [shape(8, 2, wrows, wide_cols), shape(8, 2, wrows, wide_cols)]
+        else:
+            outs.append(shape(width, wide_cols, dtype=WIDE))
+        keep, send, *carried = call(
+            functools.partial(attend_back_kernel, size, seq),
+            tuple(outs) + (shape(8, width, dtype=WIDE),),
+            [(info, SMEM), (mine, VMEM), (other, VMEM), (w_qkv, VMEM), (gain_one, VMEM), (scale, VMEM)]
+            + [(grad_att, VMEM)]
+            + [(v, VMEM) for v in carried],
+            scratch,
+            flops=6 * 8 * rows * width * wide_cols,
+        )
+        parts += scatter_seq(info, keep, send)
+    half_keep, half_send, sums_att = carried
+    grad_tokens = call(
+        tokens_kernel,
+        shape(seq_count, rows, width, dtype=WIDE),
+        [(tokens, VMEM), (gain_one, VMEM), (grad_hidden.reshape(seq_count, rows, width), VMEM)]
+        + [(v, VMEM) for v in parts],
+    )
+
+    half = half_keep.astype(WIDE) + swap(half_send, "grp", 1, 4).astype(WIDE)
+    part = lax.dynamic_index_in_dim(half, x, 1, keepdims=False)
+    far = lax.dynamic_index_in_dim(half, 1 - x, 1, keepdims=False).astype(LOW)
+    part = part + swap(far, "grp", 2, 4).astype(WIDE)
+    part = lax.all_to_all(part.astype(LOW), "seq", 0, 0, tiled=True)
+    qkv_grads = call(
+        functools.partial(rows_kernel, share),
+        (whole, whole, whole),
+        [(info, SMEM)] + [(v, VMEM) for v in over_grp(part)],
+    )
+
+    sums = jnp.concatenate([sums_att[:2], sums_ff[:3], sums_ff[5:8]], 0)
+    for axis, bit, length in (("grp", 1, 4), ("grp", 2, 4), ("seq", 1, 8), ("seq", 2, 8), ("seq", 4, 8)):
+        sums = sums + swap(sums, axis, bit, length)
+    grad_scale = sums[1, :size] * factor * jax.nn.sigmoid(query_scale)
+    return (
+        layer_out.reshape(seq_count, rows, width),
+        grad_tokens,
+        *qkv_grads,
+        *ff_grads,
+        sums[0],
+        sums[2],
+        sums[3],
+        sums[4],
+        grad_scale,
+    )
+
+
 def solution(mesh):
+    fits = mesh.shape["grp"] == 4 and mesh.shape["seq"] == 8
     return jax.shard_map(
-        shards,
+        quick if fits else shards,
         mesh=mesh,
         in_specs=(
             P("grp", "seq", None),

time: 1480 us -> 350 us (0.24)
  waiting for transfers between devices: 1130 us -> 136 us
  blocking collectives: 139 us -> 0 us
  starting transfers between devices: 1.15 us -> 95.7 us
  matrix products: 94.3 us -> 0 us
  Pallas kernels: 0 us -> 52.8 us
  local copies, waits for them, and re-layouts: 69.9 us -> 39.9 us
  between operations: 16.3 us -> 0.98 us
    reduce_scatter x6 -> x0, waiting for transfers between devices: 697 us -> none  [the longest x1 125 us: shards(): lax.psum_scatter(grads[3], 'seq', scatter_dimension=0, tiled=True)]
    all_gather x10 -> x0, waiting for transfers between devices: 376 us -> none  [the longest x1 58.5 us: shards(): lax.all_gather(params[5], ('grp', 'seq'), axis=0, tiled=True)]
    ppermute x0 -> x59, waiting for transfers between devices: none -> 130 us  [swap(): return lax.ppermute(value, axis, [(i, i ^ bit) for i in range(size)])]
    dot_general x27 -> x0, matrix products: 94.3 us -> none  [the longest x4 14.4 us: masked_scores(): jnp.einsum('sqhe,skhe->shqk', heads_of(query_rows, head_size), heads_of(k...]
    ppermute x0 -> x59, starting transfers between devices: none -> 74 us  [swap(): return lax.ppermute(value, axis, [(i, i ^ bit) for i in range(size)])]
    all_gather x2 -> x0, blocking collectives: 56.1 us -> none  [the longest x1 28.7 us: shards(): lax.all_gather(delta, 'seq', axis=2, tiled=True)]
    pallas_call x0 -> x12, Pallas kernels: none -> 52.8 us  [call(): pl.pallas_call(body, out_shape=outs, in_specs=[spec for _, spec in ins],...]
    psum x1 -> x0, waiting for transfers between devices: 49.7 us -> none  [shards(): lax.psum((shares[0], shares[1], shares[2], shares[3], shares[4], shares[5...]
  transfers between devices with their start and end apart: 17 -> 63, of which waited for: 15 -> 16; matrix products, arithmetic and copies ran while one was open for 12% -> 13% of each run, Pallas kernels for 0% -> 12%
where the time goes in v2:
time: 350 us; the launch traced here: 344 us
  waiting for transfers between devices  136 us (39%)
  starting transfers between devices  95.7 us (27%)
  Pallas kernels  52.8 us (15%)
  local copies, waits for them, and re-layouts  39.9 us (11%)
  other arithmetic  18.7 us (5%)
    ppermute x59, waiting for transfers between devices, swap(): return lax.ppermute(value, axis, [(i, i ^ bit) for i in range(size)])  130 us
    ppermute x59, starting transfers between devices, swap(): return lax.ppermute(value, axis, [(i, i ^ bit) for i in range(size)])  74 us
    pallas_call x12, Pallas kernels, call(): pl.pallas_call(body, out_shape=outs, in_specs=[spec for _, spec in ins],...  52.8 us
    ppermute x9, local copies, waits for them, and re-layouts, swap(): return lax.ppermute(value, axis, [(i, i ^ bit) for i in range(size)])  17.2 us
    unnamed x71, local copies, waits for them, and re-layouts  12.4 us
  transfers between devices with their start and end apart: 63, of which 16 were waited for; matrix products, arithmetic and copies ran while one was open for 13% of the time, Pallas kernels for 12%

profile of v2, /device:TPU:9, one launch (start us, length us, event | category | flops | bytes accessed | tf_op | source)
XLA Modules:
  0.0 343.9 jit_solution(13011920301504845290)
XLA Ops:
  0.7 1.4 collective-permute-start.14
  7.5 1.3 collective-permute-done.14
  12.4 5.7 %all-to-all-start = ((bf16[8,40,512]{2,1,0:T(8,128)(2,1)}), bf16[8,40,512]{2,1,0:T(8,128)(2,1)S(1)}, u32[]{:S(2)}, u32[]{:S(2)}) async-start(bf16[8,40,512]{2,1,0:T(8,128)(2,1)} %shard_map.237), calls=%async_computation | async-start | bytes 655360 | tf_op jit(solution)/shard_map/all_to_all | solution.py:735
  25.6 21.9 %collective-permute-done.7 = bf16[40,1280]{1,0:T(8,128)(2,1)S(1)} collective-permute-done((bf16[40,1280]{1,0:T(8,128)(2,1)S(1)}, bf16[40,1280]{1,0:T(8,128)(2,1)S(1)}, u32[]{:S(2)}, u32[]{:S(2)}) %collective-permute-start.7) | collective-permute-done | bytes 102432 | tf_op jit(solution)/shard_map/ppermute | solution.py:373
  47.5 1.5 collective-permute-done.8
  51.3 5.6 %collective-permute-done = bf16[2,64,1280]{2,1,0:T(8,128)(2,1)S(1)} collective-permute-done((bf16[2,64,1280]{2,1,0:T(8,128)(2,1)S(1)}, bf16[2,64,1280]{2,1,0:T(8,128)(2,1)S(1)}, u32[]{:S(2)}, u32[]{:S(2)}) %collective-permute-start) | collective-permute-done | bytes 327712 | tf_op jit(solution)/shard_map/ppermute | solution.py:373
  56.9 1.3 collective-permute-start.10
  58.2 4.8 %collective-permute-done.1 = bf16[2,64,1280]{2,1,0:T(8,128)(2,1)S(1)} collective-permute-done((bf16[2,64,1280]{2,1,0:T(8,128)(2,1)S(1)}, bf16[2,64,1280]{2,1,0:T(8,128)(2,1)S(1)}, u32[]{:S(2)}, u32[]{:S(2)}) %collective-permute-start.1) | collective-permute-done | bytes 327712 | tf_op jit(solution)/shard_map/ppermute | solution.py:373
  63.2 1.3 collective-permute-start.4
  66.9 2.2 maximum_select_fusion.1
  69.3 3.8 %collective-permute-start.6 = (bf16[8,40,512]{2,1,0:T(8,128)(2,1)S(1)}, bf16[8,40,512]{2,1,0:T(8,128)(2,1)}, u32[]{:S(2)}, u32[]{:S(2)}) collective-permute-start(bf16[8,40,512]{2,1,0:T(8,128)(2,1)S(1)} %all-to-all-done), channel_id=1, source_target_pairs={{0,8},{8,0},{16,24},{24,16},{1,9},{9,1},{17,25},{25,17},{2,10},{10... | collective-permute-start | bytes 983048 | tf_op jit(solution)/shard_map/ppermute | solution.py:373
  74.3 2.2 maximum_select_fusion.2
  76.5 2.2 collective-permute-start.26
  78.6 2.1 maximum_select_fusion
  80.8 4.8 %collective-permute-start.18 = (bf16[4,2,40,1280]{3,2,0,1:T(8,128)(2,1)}, bf16[4,2,40,1280]{3,2,0,1:T(8,128)(2,1)}, u32[]{:S(2)}, u32[]{:S(2)}) collective-permute-start(bf16[4,2,40,1280]{3,2,0,1:T(8,128)(2,1)} %maximum_select_fusion.1), channel_id=1, source_target_pairs={{0,8},{8,0},{16,24},{24,16},{1,9},{9,1},{17,25},{25,17},{2,10},{10... | collective-permute-start | bytes 2457608 | tf_op jit(solution)/shard_map/ppermute | solution.py:373
  86.7 1.3 select_bitcast_fusion.3
  89.0 3.7 %collective-permute-start.25 = (bf16[4,2,40,1280]{3,2,0,1:T(8,128)(2,1)}, bf16[4,2,40,1280]{3,2,0,1:T(8,128)(2,1)}, u32[]{:S(2)}, u32[]{:S(2)}) collective-permute-start(bf16[4,2,40,1280]{3,2,0,1:T(8,128)(2,1)} %maximum_select_fusion.2), channel_id=1, source_target_pairs={{0,8},{8,0},{16,24},{24,16},{1,9},{9,1},{17,25},{25,17},{2,10},{10... | collective-permute-start | bytes 2457608 | tf_op jit(solution)/shard_map/ppermute | solution.py:373
  92.7 13.9 %collective-permute-done.26 = bf16[4,2,40,1280]{3,2,0,1:T(8,128)(2,1)} collective-permute-done((bf16[4,2,40,1280]{3,2,0,1:T(8,128)(2,1)}, bf16[4,2,40,1280]{3,2,0,1:T(8,128)(2,1)}, u32[]{:S(2)}, u32[]{:S(2)}) %collective-permute-start.26) | collective-permute-done | bytes 819232 | tf_op jit(solution)/shard_map/ppermute | solution.py:373
  106.5 3.7 %collective-permute-start.11 = (bf16[4,2,40,1280]{3,2,0,1:T(8,128)(2,1)}, bf16[4,2,40,1280]{3,2,0,1:T(8,128)(2,1)}, u32[]{:S(2)}, u32[]{:S(2)}) collective-permute-start(bf16[4,2,40,1280]{3,2,0,1:T(8,128)(2,1)} %maximum_select_fusion), channel_id=1, source_target_pairs={{0,8},{8,0},{16,24},{24,16},{1,9},{9,1},{17,25},{25,17},{2,10},{10... | collective-permute-start | bytes 2457608 | tf_op jit(solution)/shard_map/ppermute | solution.py:373
  110.2 13.8 %collective-permute-done.12 = bf16[4,2,40,1280]{3,2,0,1:T(8,128)(2,1)} collective-permute-done((bf16[4,2,40,1280]{3,2,0,1:T(8,128)(2,1)}, bf16[4,2,40,1280]{3,2,0,1:T(8,128)(2,1)}, u32[]{:S(2)}, u32[]{:S(2)}) %collective-permute-start.12) | collective-permute-done | bytes 819232 | tf_op jit(solution)/shard_map/ppermute | solution.py:373
  124.1 2.1 collective-permute-start.27
  127.4 1.3 copy.87
  128.7 7.8 %shard_map.238 = bf16[8,2,64,160]{3,2,1,0:T(8,128)(2,1)} custom-call(s32[8]{0:T(128)S(1)} %stack.159.info, bf16[4,2,64,1280]{3,2,1,0:T(8,128)(2,1)} %pad_maximum_fusion.mine, bf16[4,2,64,1280]{3,2,1,0:T(8,128)(2,1)S(1)} %collective-permute-done.3.other, bf16[1280,512]{1,0:T(8,128)(2,1)S(1)} %bitcast.97, f32[1,1280]{1,0:T(1,128)S(1)} %slice.44.gain, ...), custom_call_target="tpu_custom_call" | custom-call | flops 1342177280 | bytes 3937632 | tf_op jit(solution)/shard_map/pallas_call | solution.py:416
  136.5 6.5 %all-to-all-start.1 = ((bf16[8,2,64,160]{3,2,1,0:T(8,128)(2,1)}), bf16[8,2,64,160]{3,2,1,0:T(8,128)(2,1)S(1)}, u32[]{:S(2)}, u32[]{:S(2)}) async-start(bf16[8,2,64,160]{3,2,1,0:T(8,128)(2,1)} %shard_map.238), calls=%async_computation.1 | async-start | bytes 1048576 | tf_op jit(solution)/shard_map/all_to_all | solution.py:754
  143.0 2.1 copy.74
  145.1 2.1 copy.78
  148.3 2.1 copy.76
  150.4 2.2 copy.80
  153.8 2.1 copy.75
  155.9 2.1 copy.79
  159.3 2.1 copy.77
  161.3 2.1 copy.81
  163.4 2.1 copy.73
  166.5 9.2 %shard_map.239 = (bf16[128,1280]{1,0:T(8,128)(2,1)}, f32[128,1280]{1,0:T(8,128)S(1)}, bf16[8,128,160]{2,1,0:T(8,128)(2,1)S(1)}, bf16[128,3840]{1,0:T(8,128)(2,1)...) custom-call(s32[8]{0:T(128)S(1)} %stack.159.info, ...), custom_call_target="tpu_custom_call" | custom-call | flops 2936012800 | bytes 10833952 | tf_op jit(solution)/shard_map/pallas_call | solution.py:416
  178.1 2.1 copy.82
  180.2 5.5 %all-to-all-start.2 = ((bf16[8,128,160]{1,2,0:T(8,128)(2,1)}), bf16[8,128,160]{1,2,0:T(8,128)(2,1)S(1)}, u32[]{:S(2)}, u32[]{:S(2)}) async-start(bf16[8,128,160]{1,2,0:T(8,128)(2,1)} %copy.82), calls=%async_computation.2 | async-start | bytes 655360 | tf_op jit(solution)/shard_map/all_to_all | solution.py:778
  186.9 6.0 %all-to-all-done.2 = bf16[8,128,160]{1,2,0:T(8,128)(2,1)S(1)} async-done(((bf16[8,128,160]{1,2,0:T(8,128)(2,1)}), bf16[8,128,160]{1,2,0:T(8,128)(2,1)S(1)}, u32[]{:S(2)}, u32[]{:S(2)}) %all-to-all-start.2) | async-done | bytes 327712 | tf_op jit(solution)/shard_map/all_to_all | solution.py:778
  193.1 1.3 copy-done.18
  194.4 8.5 %shard_map.240 = (bf16[4,64,1280]{2,1,0:T(8,128)(2,1)S(1)}, bf16[4,64,1280]{2,1,0:T(8,128)(2,1)}, f32[1280,512]{1,0:T(8,128)}, f32[8,1280]{1,0:T(8,128)S(1)}) custom-call(s32[8]{0:T(128)S(1)} %stack.159.info, bf16[4,2,64,1280]{3,2,1,0:T(8,128)(2,1)} %pad_maximum_fusion.mine, bf16[4,2,64,1280]{3,2,1,0:T(8,128)(2,1)S(1)} %copy-done.18, ...), custom_call_target="tpu_custom_call" | custom-call | flops 2013265920 | bytes 4265312 | tf_op jit(solution)/shard_map/pallas_call | solution.py:416
  203.7 9.1 %shard_map.242 = (bf16[4,64,1280]{2,1,0:T(8,128)(2,1)S(1)}, bf16[4,64,1280]{2,1,0:T(8,128)(2,1)}, bf16[8,2,40,512]{3,2,1,0:T(8,128)(2,1)S(1)}, bf16[8,2,40,512]{3,2,1,0:T(8,128)(2,1)S(1)}, f32[8,1280]{1,0:T(8,128)S(1)}) custom-call(s32[8]{0:T(128)S(1)} %stack.159.info, bf16[4,2,64,1280]{3,2,1,0:T(8,128)(2,1)} %pad_maximum_fusion.mine, ...), custom_call_target="tpu_custom_call" | custom-call | flops 2013265920 | bytes 6927712 | tf_op jit(solution)/shard_map/pallas_call | solution.py:416
  214.3 3.3 collective-permute-start.36
  219.7 10.8 %collective-permute-done.45.refs_6_ = bf16[128,1920]{1,0:T(8,128)(2,1)S(1)} collective-permute-done((bf16[128,1920]{1,0:T(8,128)(2,1)S(1)}, bf16[128,1920]{1,0:T(8,128)(2,1)S(1)}, u32[]{:S(2)}, u32[]{:S(2)}) %collective-permute-start.45) | collective-permute-done | bytes 491552 | tf_op jit(solution)/shard_map/ppermute | solution.py:373
  231.3 1.3 convert_add_fusion
  232.7 1.3 collective-permute-start.37
  234.0 6.1 %shard_map.246 = (bf16[4,160,960]{2,1,0:T(8,128)(2,1)}, bf16[4,160,960]{2,1,0:T(8,128)(2,1)}) custom-call(s32[8]{0:T(128)S(1)} %stack.159.info, bf16[128,3840]{1,0:T(8,128)(2,1)S(1)} %copy-done.4, bf16[128,3840]{1,0:T(8,128)(2,1)} %collective-permute-done.41.refs_1_, bf16[128,3840]{1,0:T(8,128)(2,1)S(1)} %collective-permute-done.42.refs_2_, ...), custom_call_target="tpu_custom_call" | custom-call | flops 1258291200 | bytes 5898272 | tf_op jit(solution)/shard_map/pallas_call | solution.py:416
  241.5 1.5 collective-permute-start.32
  243.8 4.1 %all-to-all-start.3 = ((bf16[8,40,512]{2,1,0:T(8,128)(2,1)}), bf16[8,40,512]{2,1,0:T(8,128)(2,1)S(1)}, u32[]{:S(2)}, u32[]{:S(2)}) async-start(bf16[8,40,512]{2,1,0:T(8,128)(2,1)} %fusion), calls=%async_computation.3 | async-start | bytes 655360 | tf_op jit(solution)/shard_map/all_to_all | solution.py:827
  248.3 3.0 collective-permute-done.55
  252.5 20.6 %collective-permute-done.47.received = bf16[4,160,960]{2,1,0:T(8,128)(2,1)} collective-permute-done((bf16[4,160,960]{2,1,0:T(8,128)(2,1)}, bf16[4,160,960]{2,1,0:T(8,128)(2,1)}, u32[]{:S(2)}, u32[]{:S(2)}) %collective-permute-start.47) | collective-permute-done | bytes 1228832 | tf_op jit(solution)/shard_map/ppermute | solution.py:373
  273.1 2.3 shard_map.247
  278.0 10.8 %collective-permute-done.56 = f32[8,1280]{1,0:T(8,128)S(1)} collective-permute-done((f32[8,1280]{1,0:T(8,128)S(1)}, f32[8,1280]{1,0:T(8,128)S(1)}, u32[]{:S(2)}, u32[]{:S(2)}) %collective-permute-start.56) | collective-permute-done | bytes 40992 | tf_op jit(solution)/shard_map/ppermute | solution.py:373
  289.0 1.8 collective-permute-start.57
  290.8 1.4 shard_map.243
  293.6 1.4 collective-permute-start.34
  295.0 11.7 %collective-permute-done.50 = bf16[160,960]{1,0:T(8,128)(2,1)} collective-permute-done((bf16[160,960]{1,0:T(8,128)(2,1)}, bf16[160,960]{1,0:T(8,128)(2,1)}, u32[]{:S(2)}, u32[]{:S(2)}) %collective-permute-start.50) | collective-permute-done | bytes 307232 | tf_op jit(solution)/shard_map/ppermute | solution.py:373
  307.0 1.4 add_convert_fusion.a
  308.4 1.3 collective-permute-start.52
  311.3 3.1 collective-permute-done.58
  314.7 1.7 collective-permute-start.29
  317.1 6.2 %collective-permute-done.35.refs_7_ = bf16[64,1280]{1,0:T(8,128)(2,1)S(1)} collective-permute-done((bf16[64,1280]{1,0:T(8,128)(2,1)S(1)}, bf16[64,1280]{1,0:T(8,128)(2,1)S(1)}, u32[]{:S(2)}, u32[]{:S(2)}) %collective-permute-start.35) | collective-permute-done | bytes 163872 | tf_op jit(solution)/shard_map/ppermute | solution.py:373
  323.3 11.2 %collective-permute-start.38 = (bf16[8,40,512]{2,1,0:T(8,128)(2,1)S(1)}, bf16[8,40,512]{2,1,0:T(8,128)(2,1)S(1)}, u32[]{:S(2)}, u32[]{:S(2)}) collective-permute-start(bf16[8,40,512]{2,1,0:T(8,128)(2,1)S(1)} %all-to-all-done.3.a), channel_id=1, source_target_pairs={{0,8},{8,0},{16,24},{24,16},{1,9},{9,1},{17,25},{25,17},{2,10},{10... | collective-permute-start | bytes 983048 | tf_op jit(solution)/shard_map/ppermute | solution.py:373
  337.0 2.2 shard_map.244
  339.2 2.4 shard_map.245
  341.5 2.4 shard_map.248
  (193 shorter events, 53.1 us)
Async XLA Ops:
  0.7 8.1 %collective-permute-start.14 = (bf16[40,1280]{1,0:T(8,128)(2,1)}, bf16[40,1280]{1,0:T(8,128)(2,1)S(1)}, u32[]{:S(2)}, u32[]{:S(2)}) collective-permute-start(bf16[40,1280]{1,0:T(8,128)(2,1)} %param.20), channel_id=1, source_target_pairs={{0,6},{1,7},{2,4},{3,5},{4,2},{5,3},{6,0},{7,1},{8,14},{9,15},{10,... | collective-permute-start | bytes 307208 | tf_op jit(solution)/shard_map/ppermute | solution.py:373
  2.0 16.0 %collective-permute-start.15 = (bf16[40,1280]{1,0:T(8,128)(2,1)}, bf16[40,1280]{1,0:T(8,128)(2,1)S(1)}, u32[]{:S(2)}, u32[]{:S(2)}) collective-permute-start(bf16[40,1280]{1,0:T(8,128)(2,1)} %param.20), channel_id=1, source_target_pairs={{0,4},{1,5},{2,6},{3,7},{4,0},{5,1},{6,2},{7,3},{8,12},{9,13},{10,... | collective-permute-start | bytes 307208 | tf_op jit(solution)/shard_map/ppermute | solution.py:373
  3.1 16.2 %collective-permute-start.16 = (bf16[40,1280]{1,0:T(8,128)(2,1)}, bf16[40,1280]{1,0:T(8,128)(2,1)S(1)}, u32[]{:S(2)}, u32[]{:S(2)}) collective-permute-start(bf16[40,1280]{1,0:T(8,128)(2,1)} %param.20), channel_id=1, source_target_pairs={{0,2},{1,3},{2,0},{3,1},{4,6},{5,7},{6,4},{7,5},{8,10},{9,11},{10,... | collective-permute-start | bytes 307208 | tf_op jit(solution)/shard_map/ppermute | solution.py:373
  4.2 16.1 %collective-permute-start.21 = (bf16[40,1280]{1,0:T(8,128)(2,1)}, bf16[40,1280]{1,0:T(8,128)(2,1)S(1)}, u32[]{:S(2)}, u32[]{:S(2)}) collective-permute-start(bf16[40,1280]{1,0:T(8,128)(2,1)} %param.21), channel_id=1, source_target_pairs={{0,6},{1,7},{2,4},{3,5},{4,2},{5,3},{6,0},{7,1},{8,14},{9,15},{10,... | collective-permute-start | bytes 307208 | tf_op jit(solution)/shard_map/ppermute | solution.py:373
  5.4 16.1 %collective-permute-start.22 = (bf16[40,1280]{1,0:T(8,128)(2,1)}, bf16[40,1280]{1,0:T(8,128)(2,1)S(1)}, u32[]{:S(2)}, u32[]{:S(2)}) collective-permute-start(bf16[40,1280]{1,0:T(8,128)(2,1)} %param.21), channel_id=1, source_target_pairs={{0,4},{1,5},{2,6},{3,7},{4,0},{5,1},{6,2},{7,3},{8,12},{9,13},{10,... | collective-permute-start | bytes 307208 | tf_op jit(solution)/shard_map/ppermute | solution.py:373
  8.7 13.9 %collective-permute-start.23 = (bf16[40,1280]{1,0:T(8,128)(2,1)}, bf16[40,1280]{1,0:T(8,128)(2,1)S(1)}, u32[]{:S(2)}, u32[]{:S(2)}) collective-permute-start(bf16[40,1280]{1,0:T(8,128)(2,1)} %param.21), channel_id=1, source_target_pairs={{0,2},{1,3},{2,0},{3,1},{4,6},{5,7},{6,4},{7,5},{8,10},{9,11},{10,... | collective-permute-start | bytes 307208 | tf_op jit(solution)/shard_map/ppermute | solution.py:373
  12.4 50.8 %all-to-all-start = ((bf16[8,40,512]{2,1,0:T(8,128)(2,1)}), bf16[8,40,512]{2,1,0:T(8,128)(2,1)S(1)}, u32[]{:S(2)}, u32[]{:S(2)}) async-start(bf16[8,40,512]{2,1,0:T(8,128)(2,1)} %shard_map.237), calls=%async_computation | async-start | bytes 655360 | tf_op jit(solution)/shard_map/all_to_all | solution.py:735
  18.0 29.5 %collective-permute-start.7 = (bf16[40,1280]{1,0:T(8,128)(2,1)S(1)}, bf16[40,1280]{1,0:T(8,128)(2,1)S(1)}, u32[]{:S(2)}, u32[]{:S(2)}) collective-permute-start(bf16[40,1280]{1,0:T(8,128)(2,1)S(1)} %copy-done.32), channel_id=1, source_target_pairs={{0,6},{1,7},{2,4},{3,5},{4,2},{5,3},{6,0},{7,1},{8,14},{9,15},{10,... | collective-permute-start | bytes 307208 | tf_op jit(solution)/shard_map/ppermute | solution.py:373
  19.3 29.7 %collective-permute-start.8 = (bf16[40,1280]{1,0:T(8,128)(2,1)S(1)}, bf16[40,1280]{1,0:T(8,128)(2,1)S(1)}, u32[]{:S(2)}, u32[]{:S(2)}) collective-permute-start(bf16[40,1280]{1,0:T(8,128)(2,1)S(1)} %copy-done.32), channel_id=1, source_target_pairs={{0,4},{1,5},{2,6},{3,7},{4,0},{5,1},{6,2},{7,3},{8,12},{9,13},{10,... | collective-permute-start | bytes 307208 | tf_op jit(solution)/shard_map/ppermute | solution.py:373
  20.3 29.9 %collective-permute-start.9 = (bf16[40,1280]{1,0:T(8,128)(2,1)S(1)}, bf16[40,1280]{1,0:T(8,128)(2,1)S(1)}, u32[]{:S(2)}, u32[]{:S(2)}) collective-permute-start(bf16[40,1280]{1,0:T(8,128)(2,1)S(1)} %copy-done.32), channel_id=1, source_target_pairs={{0,2},{1,3},{2,0},{3,1},{4,6},{5,7},{6,4},{7,5},{8,10},{9,11},{10,... | collective-permute-start | bytes 307208 | tf_op jit(solution)/shard_map/ppermute | solution.py:373
  21.5 35.4 %collective-permute-start = (bf16[2,64,1280]{2,1,0:T(8,128)(2,1)S(1)}, bf16[2,64,1280]{2,1,0:T(8,128)(2,1)S(1)}, u32[]{:S(2)}, u32[]{:S(2)}) collective-permute-start(bf16[2,64,1280]{2,1,0:T(8,128)(2,1)S(1)} %copy-done), channel_id=1, source_target_pairs={{0,6},{1,7},{2,4},{3,5},{4,2},{5,3},{6,0},{7,1},{8,14},{9,15},{10,... | collective-permute-start | bytes 983048 | tf_op jit(solution)/shard_map/ppermute | solution.py:373
  22.7 40.4 %collective-permute-start.1 = (bf16[2,64,1280]{2,1,0:T(8,128)(2,1)S(1)}, bf16[2,64,1280]{2,1,0:T(8,128)(2,1)S(1)}, u32[]{:S(2)}, u32[]{:S(2)}) collective-permute-start(bf16[2,64,1280]{2,1,0:T(8,128)(2,1)S(1)} %copy-done), channel_id=1, source_target_pairs={{0,4},{1,5},{2,6},{3,7},{4,0},{5,1},{6,2},{7,3},{8,12},{9,13},{10,... | collective-permute-start | bytes 983048 | tf_op jit(solution)/shard_map/ppermute | solution.py:373
  47.5 15.5 %collective-permute-start.2 = (bf16[2,64,1280]{2,1,0:T(8,128)(2,1)S(1)}, bf16[2,64,1280]{2,1,0:T(8,128)(2,1)S(1)}, u32[]{:S(2)}, u32[]{:S(2)}) collective-permute-start(bf16[2,64,1280]{2,1,0:T(8,128)(2,1)S(1)} %copy-done), channel_id=1, source_target_pairs={{0,2},{1,3},{2,0},{3,1},{4,6},{5,7},{6,4},{7,5},{8,10},{9,11},{10,... | collective-permute-start | bytes 983048 | tf_op jit(solution)/shard_map/ppermute | solution.py:373
  49.0 17.9 %collective-permute-start.17 = (bf16[4,40,1280]{2,1,0:T(8,128)(2,1)}, bf16[4,40,1280]{2,1,0:T(8,128)(2,1)}, u32[]{:S(2)}, u32[]{:S(2)}) collective-permute-start(bf16[4,40,1280]{2,1,0:T(8,128)(2,1)} %get-tuple-element.104), channel_id=1, source_target_pairs={{0,1},{1,0},{2,3},{3,2},{4,5},{5,4},{6,7},{7,6},{8,9},{9,8},{10,11... | collective-permute-start | bytes 1228808 | tf_op jit(solution)/shard_map/ppermute | solution.py:373
  50.2 19.1 %collective-permute-start.24 = (bf16[4,40,1280]{2,1,0:T(8,128)(2,1)}, bf16[4,40,1280]{2,1,0:T(8,128)(2,1)}, u32[]{:S(2)}, u32[]{:S(2)}) collective-permute-start(bf16[4,40,1280]{2,1,0:T(8,128)(2,1)} %get-tuple-element.98), channel_id=1, source_target_pairs={{0,1},{1,0},{2,3},{3,2},{4,5},{5,4},{6,7},{7,6},{8,9},{9,8},{10,11... | collective-permute-start | bytes 1228808 | tf_op jit(solution)/shard_map/ppermute | solution.py:373
  56.9 19.6 %collective-permute-start.10 = (bf16[4,40,1280]{2,1,0:T(8,128)(2,1)}, bf16[4,40,1280]{2,1,0:T(8,128)(2,1)}, u32[]{:S(2)}, u32[]{:S(2)}) collective-permute-start(bf16[4,40,1280]{2,1,0:T(8,128)(2,1)} %get-tuple-element.110), channel_id=1, source_target_pairs={{0,1},{1,0},{2,3},{3,2},{4,5},{5,4},{6,7},{7,6},{8,9},{9,8},{10,11... | collective-permute-start | bytes 1228808 | tf_op jit(solution)/shard_map/ppermute | solution.py:373
  63.2 10.0 %collective-permute-start.4 = (bf16[8,40,512]{2,1,0:T(8,128)(2,1)S(1)}, bf16[8,40,512]{2,1,0:T(8,128)(2,1)S(1)}, u32[]{:S(2)}, u32[]{:S(2)}) collective-permute-start(bf16[8,40,512]{2,1,0:T(8,128)(2,1)S(1)} %all-to-all-done), channel_id=1, source_target_pairs={{0,16},{8,24},{16,0},{24,8},{1,17},{9,25},{17,1},{25,9},{2,18},{10... | collective-permute-start | bytes 983048 | tf_op jit(solution)/shard_map/ppermute | solution.py:373
  65.7 60.5 %collective-permute-start.3 = (bf16[4,2,64,1280]{3,2,1,0:T(8,128)(2,1)}, bf16[4,2,64,1280]{3,2,1,0:T(8,128)(2,1)S(1)}, u32[]{:S(2)}, u32[]{:S(2)}) collective-permute-start(bf16[4,2,64,1280]{3,2,1,0:T(8,128)(2,1)} %pad_maximum_fusion.mine), channel_id=1, source_target_pairs={{0,1},{1,0},{2,3},{3,2},{4,5},{5,4},{6,7},{7,6},{8,9},{9,8},{10,11... | collective-permute-start | bytes 3932168 | tf_op jit(solution)/shard_map/ppermute | solution.py:373
  69.1 19.9 %collective-permute-start.19 = (bf16[4,2,40,1280]{3,2,0,1:T(8,128)(2,1)}, bf16[4,2,40,1280]{3,2,0,1:T(8,128)(2,1)}, u32[]{:S(2)}, u32[]{:S(2)}) collective-permute-start(bf16[4,2,40,1280]{3,2,0,1:T(8,128)(2,1)} %maximum_select_fusion.1), channel_id=1, source_target_pairs={{0,16},{8,24},{16,0},{24,8},{1,17},{9,25},{17,1},{25,9},{2,18},{10... | collective-permute-start | bytes 2457608 | tf_op jit(solution)/shard_map/ppermute | solution.py:373
  69.3 11.5 %collective-permute-start.6 = (bf16[8,40,512]{2,1,0:T(8,128)(2,1)S(1)}, bf16[8,40,512]{2,1,0:T(8,128)(2,1)}, u32[]{:S(2)}, u32[]{:S(2)}) collective-permute-start(bf16[8,40,512]{2,1,0:T(8,128)(2,1)S(1)} %all-to-all-done), channel_id=1, source_target_pairs={{0,8},{8,0},{16,24},{24,16},{1,9},{9,1},{17,25},{25,17},{2,10},{10... | collective-permute-start | bytes 983048 | tf_op jit(solution)/shard_map/ppermute | solution.py:373
  73.2 12.4 %collective-permute-start.5 = (bf16[8,40,512]{2,1,0:T(8,128)(2,1)S(1)}, bf16[8,40,512]{2,1,0:T(8,128)(2,1)S(1)}, u32[]{:S(2)}, u32[]{:S(2)}) collective-permute-start(bf16[8,40,512]{2,1,0:T(8,128)(2,1)S(1)} %collective-permute-done.4), channel_id=1, source_target_pairs={{0,8},{8,0},{16,24},{24,16},{1,9},{9,1},{17,25},{25,17},{2,10},{10... | collective-permute-start | bytes 983048 | tf_op jit(solution)/shard_map/ppermute | solution.py:373
  76.5 30.1 %collective-permute-start.26 = (bf16[4,2,40,1280]{3,2,0,1:T(8,128)(2,1)}, bf16[4,2,40,1280]{3,2,0,1:T(8,128)(2,1)}, u32[]{:S(2)}, u32[]{:S(2)}) collective-permute-start(bf16[4,2,40,1280]{3,2,0,1:T(8,128)(2,1)} %maximum_select_fusion.2), channel_id=1, source_target_pairs={{0,16},{8,24},{16,0},{24,8},{1,17},{9,25},{17,1},{25,9},{2,18},{10... | collective-permute-start | bytes 2457608 | tf_op jit(solution)/shard_map/ppermute | solution.py:373
  80.8 29.4 %collective-permute-start.18 = (bf16[4,2,40,1280]{3,2,0,1:T(8,128)(2,1)}, bf16[4,2,40,1280]{3,2,0,1:T(8,128)(2,1)}, u32[]{:S(2)}, u32[]{:S(2)}) collective-permute-start(bf16[4,2,40,1280]{3,2,0,1:T(8,128)(2,1)} %maximum_select_fusion.1), channel_id=1, source_target_pairs={{0,8},{8,0},{16,24},{24,16},{1,9},{9,1},{17,25},{25,17},{2,10},{10... | collective-permute-start | bytes 2457608 | tf_op jit(solution)/shard_map/ppermute | solution.py:373
  86.3 37.8 %collective-permute-start.12 = (bf16[4,2,40,1280]{3,2,0,1:T(8,128)(2,1)}, bf16[4,2,40,1280]{3,2,0,1:T(8,128)(2,1)}, u32[]{:S(2)}, u32[]{:S(2)}) collective-permute-start(bf16[4,2,40,1280]{3,2,0,1:T(8,128)(2,1)} %maximum_select_fusion), channel_id=1, source_target_pairs={{0,16},{8,24},{16,0},{24,8},{1,17},{9,25},{17,1},{25,9},{2,18},{10... | collective-permute-start | bytes 2457608 | tf_op jit(solution)/shard_map/ppermute | solution.py:373
  88.2 48.3 %copy-start.1 = (bf16[4,8,40,512]{3,2,1,0:T(8,128)(2,1)}, bf16[4,8,40,512]{3,2,1,0:T(8,128)(2,1)S(1)}, u32[]{:S(2)}) copy-start(bf16[4,8,40,512]{3,2,1,0:T(8,128)(2,1)S(1)} %pad_maximum_fusion.1) | copy-start | bytes 3932164
  89.0 66.9 %collective-permute-start.25 = (bf16[4,2,40,1280]{3,2,0,1:T(8,128)(2,1)}, bf16[4,2,40,1280]{3,2,0,1:T(8,128)(2,1)}, u32[]{:S(2)}, u32[]{:S(2)}) collective-permute-start(bf16[4,2,40,1280]{3,2,0,1:T(8,128)(2,1)} %maximum_select_fusion.2), channel_id=1, source_target_pairs={{0,8},{8,0},{16,24},{24,16},{1,9},{9,1},{17,25},{25,17},{2,10},{10... | collective-permute-start | bytes 2457608 | tf_op jit(solution)/shard_map/ppermute | solution.py:373
  106.5 51.5 %collective-permute-start.11 = (bf16[4,2,40,1280]{3,2,0,1:T(8,128)(2,1)}, bf16[4,2,40,1280]{3,2,0,1:T(8,128)(2,1)}, u32[]{:S(2)}, u32[]{:S(2)}) collective-permute-start(bf16[4,2,40,1280]{3,2,0,1:T(8,128)(2,1)} %maximum_select_fusion), channel_id=1, source_target_pairs={{0,8},{8,0},{16,24},{24,16},{1,9},{9,1},{17,25},{25,17},{2,10},{10... | collective-permute-start | bytes 2457608 | tf_op jit(solution)/shard_map/ppermute | solution.py:373
  110.2 49.0 %collective-permute-start.20 = (bf16[4,2,40,1280]{3,2,0,1:T(8,128)(2,1)}, bf16[4,2,40,1280]{3,2,0,1:T(8,128)(2,1)}, u32[]{:S(2)}, u32[]{:S(2)}) collective-permute-start(bf16[4,2,40,1280]{3,2,0,1:T(8,128)(2,1)} %collective-permute-done.19), channel_id=1, source_target_pairs={{0,8},{8,0},{16,24},{24,16},{1,9},{9,1},{17,25},{25,17},{2,10},{10... | collective-permute-start | bytes 2457608 | tf_op jit(solution)/shard_map/ppermute | solution.py:373
  124.1 37.3 %collective-permute-start.27 = (bf16[4,2,40,1280]{3,2,0,1:T(8,128)(2,1)}, bf16[4,2,40,1280]{3,2,0,1:T(8,128)(2,1)}, u32[]{:S(2)}, u32[]{:S(2)}) collective-permute-start(bf16[4,2,40,1280]{3,2,0,1:T(8,128)(2,1)} %collective-permute-done.26), channel_id=1, source_target_pairs={{0,8},{8,0},{16,24},{24,16},{1,9},{9,1},{17,25},{25,17},{2,10},{10... | collective-permute-start | bytes 2457608 | tf_op jit(solution)/shard_map/ppermute | solution.py:373
  126.1 37.3 %collective-permute-start.13 = (bf16[4,2,40,1280]{3,2,0,1:T(8,128)(2,1)}, bf16[4,2,40,1280]{3,2,0,1:T(8,128)(2,1)}, u32[]{:S(2)}, u32[]{:S(2)}) collective-permute-start(bf16[4,2,40,1280]{3,2,0,1:T(8,128)(2,1)} %collective-permute-done.12), channel_id=1, source_target_pairs={{0,8},{8,0},{16,24},{24,16},{1,9},{9,1},{17,25},{25,17},{2,10},{10... | collective-permute-start | bytes 2457608 | tf_op jit(solution)/shard_map/ppermute | solution.py:373
  136.5 29.1 %all-to-all-start.1 = ((bf16[8,2,64,160]{3,2,1,0:T(8,128)(2,1)}), bf16[8,2,64,160]{3,2,1,0:T(8,128)(2,1)S(1)}, u32[]{:S(2)}, u32[]{:S(2)}) async-start(bf16[8,2,64,160]{3,2,1,0:T(8,128)(2,1)} %shard_map.238), calls=%async_computation.1 | async-start | bytes 1048576 | tf_op jit(solution)/shard_map/all_to_all | solution.py:754
  180.2 12.6 %all-to-all-start.2 = ((bf16[8,128,160]{1,2,0:T(8,128)(2,1)}), bf16[8,128,160]{1,2,0:T(8,128)(2,1)S(1)}, u32[]{:S(2)}, u32[]{:S(2)}) async-start(bf16[8,128,160]{1,2,0:T(8,128)(2,1)} %copy.82), calls=%async_computation.2 | async-start | bytes 655360 | tf_op jit(solution)/shard_map/all_to_all | solution.py:778
  185.7 33.5 %collective-permute-start.42 = (bf16[128,3840]{1,0:T(8,128)(2,1)}, bf16[128,3840]{1,0:T(8,128)(2,1)S(1)}, u32[]{:S(2)}, u32[]{:S(2)}) collective-permute-start(bf16[128,3840]{1,0:T(8,128)(2,1)} %get-tuple-element.71.refs_0_), channel_id=1, source_target_pairs={{0,16},{8,24},{16,0},{24,8},{1,17},{9,25},{17,1},{25,9},{2,18},{10... | collective-permute-start | bytes 2949128 | tf_op jit(solution)/shard_map/ppermute | solution.py:373
  214.3 17.0 %collective-permute-start.36 = (bf16[8,2,40,512]{3,2,0,1:T(8,128)(2,1)}, bf16[8,2,40,512]{3,2,0,1:T(8,128)(2,1)}, u32[]{:S(2)}, u32[]{:S(2)}) collective-permute-start(bf16[8,2,40,512]{3,2,0,1:T(8,128)(2,1)} %copy.85), channel_id=1, source_target_pairs={{0,8},{8,0},{16,24},{24,16},{1,9},{9,1},{17,25},{25,17},{2,10},{10... | collective-permute-start | bytes 1966088 | tf_op jit(solution)/shard_map/ppermute | solution.py:373
  217.7 12.9 %collective-permute-start.45 = (bf16[128,1920]{1,0:T(8,128)(2,1)S(1)}, bf16[128,1920]{1,0:T(8,128)(2,1)S(1)}, u32[]{:S(2)}, u32[]{:S(2)}) collective-permute-start(bf16[128,1920]{1,0:T(8,128)(2,1)S(1)} %copy-done.21), channel_id=1, source_target_pairs={{0,16},{8,24},{16,0},{24,8},{1,17},{9,25},{17,1},{25,9},{2,18},{10... | collective-permute-start | bytes 1474568 | tf_op jit(solution)/shard_map/ppermute | solution.py:373
  218.9 15.1 %collective-permute-start.41 = (bf16[128,3840]{1,0:T(8,128)(2,1)S(1)}, bf16[128,3840]{1,0:T(8,128)(2,1)}, u32[]{:S(2)}, u32[]{:S(2)}) collective-permute-start(bf16[128,3840]{1,0:T(8,128)(2,1)S(1)} %copy-done.4), channel_id=1, source_target_pairs={{0,8},{8,0},{16,24},{24,16},{1,9},{9,1},{17,25},{25,17},{2,10},{10... | collective-permute-start | bytes 2949128 | tf_op jit(solution)/shard_map/ppermute | solution.py:373
  219.2 14.8 %collective-permute-start.43 = (bf16[128,3840]{1,0:T(8,128)(2,1)S(1)}, bf16[128,3840]{1,0:T(8,128)(2,1)}, u32[]{:S(2)}, u32[]{:S(2)}) collective-permute-start(bf16[128,3840]{1,0:T(8,128)(2,1)S(1)} %collective-permute-done.42.refs_2_), channel_id=1, source_target_pairs={{0,8},{8,0},{16,24},{24,16},{1,9},{9,1},{17,25},{25,17},{2,10},{10... | collective-permute-start | bytes 2949128 | tf_op jit(solution)/shard_map/ppermute | solution.py:373
  219.4 14.5 %collective-permute-start.44 = (bf16[128,1920]{1,0:T(8,128)(2,1)}, bf16[128,1920]{1,0:T(8,128)(2,1)}, u32[]{:S(2)}, u32[]{:S(2)}) collective-permute-start(bf16[128,1920]{1,0:T(8,128)(2,1)} %get-tuple-element.72.refs_4_), channel_id=1, source_target_pairs={{0,8},{8,0},{16,24},{24,16},{1,9},{9,1},{17,25},{25,17},{2,10},{10... | collective-permute-start | bytes 1474568 | tf_op jit(solution)/shard_map/ppermute | solution.py:373
  230.5 3.4 collective-permute-start.46
  232.7 10.3 %collective-permute-start.37 = (bf16[8,40,512]{2,1,0:T(8,128)(2,1)S(1)}, bf16[8,40,512]{2,1,0:T(8,128)(2,1)S(1)}, u32[]{:S(2)}, u32[]{:S(2)}) collective-permute-start(bf16[8,40,512]{2,1,0:T(8,128)(2,1)S(1)} %fusion.1), channel_id=1, source_target_pairs={{0,16},{8,24},{16,0},{24,8},{1,17},{9,25},{17,1},{25,9},{2,18},{10... | collective-permute-start | bytes 983048 | tf_op jit(solution)/shard_map/ppermute | solution.py:373
  240.1 33.0 %collective-permute-start.47 = (bf16[4,160,960]{2,1,0:T(8,128)(2,1)}, bf16[4,160,960]{2,1,0:T(8,128)(2,1)}, u32[]{:S(2)}, u32[]{:S(2)}) collective-permute-start(bf16[4,160,960]{2,1,0:T(8,128)(2,1)} %get-tuple-element.75), channel_id=1, source_target_pairs={{0,1},{1,0},{2,3},{3,2},{4,5},{5,4},{6,7},{7,6},{8,9},{9,8},{10,11... | collective-permute-start | bytes 3686408 | tf_op jit(solution)/shard_map/ppermute | solution.py:373
  241.0 6.9 %collective-permute-start.54 = (f32[8,1280]{1,0:T(8,128)S(1)}, f32[8,1280]{1,0:T(8,128)S(1)}, u32[]{:S(2)}, u32[]{:S(2)}) collective-permute-start(f32[8,1280]{1,0:T(8,128)S(1)} %pad_maximum_fusion.5), channel_id=1, source_target_pairs={{0,8},{8,0},{16,24},{24,16},{1,9},{9,1},{17,25},{25,17},{2,10},{10... | collective-permute-start | bytes 122888 | tf_op jit(solution)/shard_map/ppermute | solution.py:373
  241.5 47.5 %collective-permute-start.32 = (bf16[4,64,1280]{2,1,0:T(8,128)(2,1)}, bf16[4,64,1280]{2,1,0:T(8,128)(2,1)S(1)}, u32[]{:S(2)}, u32[]{:S(2)}) collective-permute-start(bf16[4,64,1280]{2,1,0:T(8,128)(2,1)} %get-tuple-element.61), channel_id=1, source_target_pairs={{0,1},{1,0},{2,3},{3,2},{4,5},{5,4},{6,7},{7,6},{8,9},{9,8},{10,11... | collective-permute-start | bytes 1966088 | tf_op jit(solution)/shard_map/ppermute | solution.py:373
  243.8 51.2 %all-to-all-start.3 = ((bf16[8,40,512]{2,1,0:T(8,128)(2,1)}), bf16[8,40,512]{2,1,0:T(8,128)(2,1)S(1)}, u32[]{:S(2)}, u32[]{:S(2)}) async-start(bf16[8,40,512]{2,1,0:T(8,128)(2,1)} %fusion), calls=%async_computation.3 | async-start | bytes 655360 | tf_op jit(solution)/shard_map/all_to_all | solution.py:827
  248.0 3.3 collective-permute-start.55
  251.3 37.5 %collective-permute-start.56 = (f32[8,1280]{1,0:T(8,128)S(1)}, f32[8,1280]{1,0:T(8,128)S(1)}, u32[]{:S(2)}, u32[]{:S(2)}) collective-permute-start(f32[8,1280]{1,0:T(8,128)S(1)} %add.67), channel_id=1, source_target_pairs={{0,1},{1,0},{2,3},{3,2},{4,5},{5,4},{6,7},{7,6},{8,9},{9,8},{10,11... | collective-permute-start | bytes 122888 | tf_op jit(solution)/shard_map/ppermute | solution.py:373
  275.4 17.4 %collective-permute-start.48 = (bf16[160,960]{1,0:T(8,128)(2,1)S(1)}, bf16[160,960]{1,0:T(8,128)(2,1)S(1)}, u32[]{:S(2)}, u32[]{:S(2)}) collective-permute-start(bf16[160,960]{1,0:T(8,128)(2,1)S(1)} %get-tuple-element.76), channel_id=1, source_target_pairs={{0,2},{1,3},{2,0},{3,1},{4,6},{5,7},{6,4},{7,5},{8,10},{9,11},{10,... | collective-permute-start | bytes 921608 | tf_op jit(solution)/shard_map/ppermute | solution.py:373
  276.1 16.7 %collective-permute-start.49 = (bf16[160,960]{1,0:T(8,128)(2,1)S(1)}, bf16[160,960]{1,0:T(8,128)(2,1)S(1)}, u32[]{:S(2)}, u32[]{:S(2)}) collective-permute-start(bf16[160,960]{1,0:T(8,128)(2,1)S(1)} %get-tuple-element.77), channel_id=1, source_target_pairs={{0,4},{1,5},{2,6},{3,7},{4,0},{5,1},{6,2},{7,3},{8,12},{9,13},{10,... | collective-permute-start | bytes 921608 | tf_op jit(solution)/shard_map/ppermute | solution.py:373
  276.8 29.9 %collective-permute-start.50 = (bf16[160,960]{1,0:T(8,128)(2,1)}, bf16[160,960]{1,0:T(8,128)(2,1)}, u32[]{:S(2)}, u32[]{:S(2)}) collective-permute-start(bf16[160,960]{1,0:T(8,128)(2,1)} %get-tuple-element.78), channel_id=1, source_target_pairs={{0,6},{1,7},{2,4},{3,5},{4,2},{5,3},{6,0},{7,1},{8,14},{9,15},{10,... | collective-permute-start | bytes 921608 | tf_op jit(solution)/shard_map/ppermute | solution.py:373
  288.8 21.7 %collective-permute-start.28 = (bf16[4,64,1280]{2,1,0:T(8,128)(2,1)}, bf16[4,64,1280]{2,1,0:T(8,128)(2,1)S(1)}, u32[]{:S(2)}, u32[]{:S(2)}) collective-permute-start(bf16[4,64,1280]{2,1,0:T(8,128)(2,1)} %get-tuple-element.53), channel_id=1, source_target_pairs={{0,1},{1,0},{2,3},{3,2},{4,5},{5,4},{6,7},{7,6},{8,9},{9,8},{10,11... | collective-permute-start | bytes 1966088 | tf_op jit(solution)/shard_map/ppermute | solution.py:373
  289.0 19.4 %collective-permute-start.57 = (f32[8,1280]{1,0:T(8,128)S(1)}, f32[8,1280]{1,0:T(8,128)}, u32[]{:S(2)}, u32[]{:S(2)}) collective-permute-start(f32[8,1280]{1,0:T(8,128)S(1)} %add.68), channel_id=1, source_target_pairs={{0,2},{1,3},{2,0},{3,1},{4,6},{5,7},{6,4},{7,5},{8,10},{9,11},{10,... | collective-permute-start | bytes 122888 | tf_op jit(solution)/shard_map/ppermute | solution.py:373
  292.8 21.9 %collective-permute-start.33 = (bf16[64,1280]{1,0:T(8,128)(2,1)}, bf16[64,1280]{1,0:T(8,128)(2,1)S(1)}, u32[]{:S(2)}, u32[]{:S(2)}) collective-permute-start(bf16[64,1280]{1,0:T(8,128)(2,1)} %get-tuple-element.63), channel_id=1, source_target_pairs={{0,2},{1,3},{2,0},{3,1},{4,6},{5,7},{6,4},{7,5},{8,10},{9,11},{10,... | collective-permute-start | bytes 491528 | tf_op jit(solution)/shard_map/ppermute | solution.py:373
  293.6 22.8 %collective-permute-start.34 = (bf16[64,1280]{1,0:T(8,128)(2,1)}, bf16[64,1280]{1,0:T(8,128)(2,1)}, u32[]{:S(2)}, u32[]{:S(2)}) collective-permute-start(bf16[64,1280]{1,0:T(8,128)(2,1)} %get-tuple-element.64), channel_id=1, source_target_pairs={{0,4},{1,5},{2,6},{3,7},{4,0},{5,1},{6,2},{7,3},{8,12},{9,13},{10,... | collective-permute-start | bytes 491528 | tf_op jit(solution)/shard_map/ppermute | solution.py:373
  306.7 27.8 %collective-permute-start.39 = (bf16[8,40,512]{2,1,0:T(8,128)(2,1)S(1)}, bf16[8,40,512]{2,1,0:T(8,128)(2,1)S(1)}, u32[]{:S(2)}, u32[]{:S(2)}) collective-permute-start(bf16[8,40,512]{2,1,0:T(8,128)(2,1)S(1)} %all-to-all-done.3.a), channel_id=1, source_target_pairs={{0,16},{8,24},{16,0},{24,8},{1,17},{9,25},{17,1},{25,9},{2,18},{10... | collective-permute-start | bytes 983048 | tf_op jit(solution)/shard_map/ppermute | solution.py:373
  308.4 27.4 %collective-permute-start.52 = (bf16[160,960]{1,0:T(8,128)(2,1)S(1)}, bf16[160,960]{1,0:T(8,128)(2,1)S(1)}, u32[]{:S(2)}, u32[]{:S(2)}) collective-permute-start(bf16[160,960]{1,0:T(8,128)(2,1)S(1)} %add_convert_fusion.a), channel_id=1, source_target_pairs={{0,16},{8,24},{16,0},{24,8},{1,17},{9,25},{17,1},{25,9},{2,18},{10... | collective-permute-start | bytes 921608 | tf_op jit(solution)/shard_map/ppermute | solution.py:373
  310.5 3.9 %collective-permute-start.58 = (f32[8,1280]{1,0:T(8,128)S(1)}, f32[8,1280]{1,0:T(8,128)S(1)}, u32[]{:S(2)}, u32[]{:S(2)}) collective-permute-start(f32[8,1280]{1,0:T(8,128)S(1)} %add.69), channel_id=1, source_target_pairs={{0,4},{1,5},{2,6},{3,7},{4,0},{5,1},{6,2},{7,3},{8,12},{9,13},{10,... | collective-permute-start | bytes 122888 | tf_op jit(solution)/shard_map/ppermute | solution.py:373
  314.4 8.9 %collective-permute-start.35 = (bf16[64,1280]{1,0:T(8,128)(2,1)S(1)}, bf16[64,1280]{1,0:T(8,128)(2,1)S(1)}, u32[]{:S(2)}, u32[]{:S(2)}) collective-permute-start(bf16[64,1280]{1,0:T(8,128)(2,1)S(1)} %copy-done.23), channel_id=1, source_target_pairs={{0,6},{1,7},{2,4},{3,5},{4,2},{5,3},{6,0},{7,1},{8,14},{9,15},{10,... | collective-permute-start | bytes 491528 | tf_op jit(solution)/shard_map/ppermute | solution.py:373
  314.7 8.6 %collective-permute-start.29 = (bf16[64,1280]{1,0:T(8,128)(2,1)S(1)}, bf16[64,1280]{1,0:T(8,128)(2,1)S(1)}, u32[]{:S(2)}, u32[]{:S(2)}) collective-permute-start(bf16[64,1280]{1,0:T(8,128)(2,1)S(1)} %get-tuple-element.55), channel_id=1, source_target_pairs={{0,2},{1,3},{2,0},{3,1},{4,6},{5,7},{6,4},{7,5},{8,10},{9,11},{10,... | collective-permute-start | bytes 491528 | tf_op jit(solution)/shard_map/ppermute | solution.py:373
  316.4 18.1 %collective-permute-start.30 = (bf16[64,1280]{1,0:T(8,128)(2,1)S(1)}, bf16[64,1280]{1,0:T(8,128)(2,1)S(1)}, u32[]{:S(2)}, u32[]{:S(2)}) collective-permute-start(bf16[64,1280]{1,0:T(8,128)(2,1)S(1)} %get-tuple-element.56), channel_id=1, source_target_pairs={{0,4},{1,5},{2,6},{3,7},{4,0},{5,1},{6,2},{7,3},{8,12},{9,13},{10,... | collective-permute-start | bytes 491528 | tf_op jit(solution)/shard_map/ppermute | solution.py:373
  323.3 13.7 %collective-permute-start.31 = (bf16[64,1280]{1,0:T(8,128)(2,1)S(1)}, bf16[64,1280]{1,0:T(8,128)(2,1)S(1)}, u32[]{:S(2)}, u32[]{:S(2)}) collective-permute-start(bf16[64,1280]{1,0:T(8,128)(2,1)S(1)} %get-tuple-element.57), channel_id=1, source_target_pairs={{0,6},{1,7},{2,4},{3,5},{4,2},{5,3},{6,0},{7,1},{8,14},{9,15},{10,... | collective-permute-start | bytes 491528 | tf_op jit(solution)/shard_map/ppermute | solution.py:373
  323.3 15.9 %collective-permute-start.38 = (bf16[8,40,512]{2,1,0:T(8,128)(2,1)S(1)}, bf16[8,40,512]{2,1,0:T(8,128)(2,1)S(1)}, u32[]{:S(2)}, u32[]{:S(2)}) collective-permute-start(bf16[8,40,512]{2,1,0:T(8,128)(2,1)S(1)} %all-to-all-done.3.a), channel_id=1, source_target_pairs={{0,8},{8,0},{16,24},{24,16},{1,9},{9,1},{17,25},{25,17},{2,10},{10... | collective-permute-start | bytes 983048 | tf_op jit(solution)/shard_map/ppermute | solution.py:373
  334.5 4.7 %collective-permute-start.40 = (bf16[8,40,512]{2,1,0:T(8,128)(2,1)S(1)}, bf16[8,40,512]{2,1,0:T(8,128)(2,1)S(1)}, u32[]{:S(2)}, u32[]{:S(2)}) collective-permute-start(bf16[8,40,512]{2,1,0:T(8,128)(2,1)S(1)} %collective-permute-done.39.c), channel_id=1, source_target_pairs={{0,8},{8,0},{16,24},{24,16},{1,9},{9,1},{17,25},{25,17},{2,10},{10... | collective-permute-start | bytes 983048 | tf_op jit(solution)/shard_map/ppermute | solution.py:373
  334.6 6.9 %collective-permute-start.51 = (bf16[160,960]{1,0:T(8,128)(2,1)S(1)}, bf16[160,960]{1,0:T(8,128)(2,1)S(1)}, u32[]{:S(2)}, u32[]{:S(2)}) collective-permute-start(bf16[160,960]{1,0:T(8,128)(2,1)S(1)} %add_convert_fusion.a), channel_id=1, source_target_pairs={{0,8},{8,0},{16,24},{24,16},{1,9},{9,1},{17,25},{25,17},{2,10},{10... | collective-permute-start | bytes 921608 | tf_op jit(solution)/shard_map/ppermute | solution.py:373
  335.8 5.7 %collective-permute-start.53 = (bf16[160,960]{1,0:T(8,128)(2,1)S(1)}, bf16[160,960]{1,0:T(8,128)(2,1)S(1)}, u32[]{:S(2)}, u32[]{:S(2)}) collective-permute-start(bf16[160,960]{1,0:T(8,128)(2,1)S(1)} %collective-permute-done.52.c), channel_id=1, source_target_pairs={{0,8},{8,0},{16,24},{24,16},{1,9},{9,1},{17,25},{25,17},{2,10},{10... | collective-permute-start | bytes 921608 | tf_op jit(solution)/shard_map/ppermute | solution.py:373
  (34 other events, 280.6 us)
